TPU v7x, 32 devices: a whole 2x2x4 slice. The times are simulated.
32 devices in a mesh: seq: 16 (over z, x, core), head: 2 (over y).
Axes of the slice: x: 2, y: 2, z: 4, core: 2. Of those that a mesh axis runs over, the one named last changes fastest.
Arguments:
- tokens: bfloat16 [2048, 3072], P('seq', 'head'), may hold values from -5 to 5, as said below
- norm_gains: float32 [5, 3072], replicated, may hold values from 0.25 to 1.75
- window: int32 [24], P('head'), may hold values from 16 to 128, as said below
- self_query: bfloat16 [3072, 3072], P(None, 'head')
- self_key_value: bfloat16 [2, 3072, 1024], P(None, None, 'head')
- self_output: bfloat16 [3072, 3072], P('head'), may hold values from -0.4375 to 0.4375
- shared_key_value: bfloat16 [2, 3072, 1024], P(None, None, 'head')
- cross_query: bfloat16 [3, 3072, 3072], P(None, 'seq', 'head')
- cross_output: bfloat16 [3, 3072, 3072], P(None, 'head', 'seq'), may hold values from -0.4375 to 0.4375
- key_blocks: int32 [3, 16, 16], P(None, 'seq'), may hold values from -1 to 15, as said below
Outputs:
- mixed: float32 [2048, 3072], P('seq', 'head')
Inputs may be any that keep to these rules, and one draw needn't show every extreme that they name: `tokens`: rows may hold near twins of the rows beside them. Some head has a window of exactly 128 and some head one of exactly 16. `key_blocks`: the row of query block b lists distinct blocks at or before b, the first being b itself; it holds min(16, b + 1) blocks and -1 in the remaining slots.
All inputs are finite; a program needn't handle non-finite values.
Results may differ from a plain program's by a relative error of at most 0.04.
Values may be sent and summed in bfloat16 or wider, within the bound.
No kernel may reach another device: no remote copies, remote signals or barrier semaphores. Data moves between devices by JAX's collectives and lax.ppermute only.
A program may use at most 192 MiB of HBM per device.

v0:
```python
import jax
import jax.numpy as jnp
from jax import lax
from jax.sharding import PartitionSpec as P

HEAD_WIDTH = 128
KEY_BLOCK_TOKENS = 128
LISTED_BLOCKS = 16
SECTIONS = 3


EPSILON = 1e-06
MASKED = -1e30


def passed_along(value, axis, steps):
    count = lax.axis_size(axis)
    initial, last = (max(0, -steps), min(count, count - steps))
    return lax.ppermute(value, axis, [(source, source + steps) for source in range(initial, last)])


def softmax_rows(scores, allowed):
    scores = jnp.where(allowed, scores, MASKED)
    largest = jnp.max(scores, axis=-1, keepdims=True)
    weights = jnp.exp(scores - largest)
    return (weights / jnp.sum(weights, axis=-1, keepdims=True)).astype(jnp.bfloat16)


def body(
    tokens,
    norm_gains,
    window,
    self_query,
    self_key_value,
    self_output,
    shared_key_value,
    cross_query,
    cross_output,
    key_blocks,
):
    seq_rank = lax.axis_index("seq")
    row_count, local_width = tokens.shape
    kv_columns = self_key_value.shape[2]
    query_columns = self_query.shape[1]
    kv_heads = kv_columns // HEAD_WIDTH
    query_group_width = query_columns // kv_columns
    scale_factor = HEAD_WIDTH ** (-0.5)

    def normed_full(stream, gain_row):
        gathered = lax.all_gather(
            stream.astype(jnp.float32).astype(jnp.bfloat16), "head", axis=1, tiled=True
        ).astype(jnp.float32)
        factor = lax.rsqrt(jnp.mean(gathered * gathered, axis=1, keepdims=True) + EPSILON)
        return (gathered * factor * gain_row[None, :]).astype(jnp.bfloat16)

    def add_branch(stream, partial_value):
        summed = lax.psum_scatter(
            partial_value.astype(jnp.bfloat16), "head", scatter_dimension=1, tiled=True
        ).astype(jnp.float32)
        return stream.astype(jnp.float32) + summed

    def project(inputs, weight):
        return jnp.dot(inputs, weight, preferred_element_type=jnp.float32).astype(jnp.bfloat16)

    first = normed_full(tokens, norm_gains[0])
    query_matrix = project(first, self_query)
    keys_own = project(first, self_key_value[0])
    values_own = project(first, self_key_value[1])
    keys_prev, values_prev = passed_along((keys_own, values_own), "seq", 1)
    near_keys = jnp.concatenate([keys_prev, keys_own], axis=0).reshape(
        2 * row_count, kv_heads, HEAD_WIDTH
    )
    near_values = jnp.concatenate([values_prev, values_own], axis=0).reshape(
        2 * row_count, kv_heads, HEAD_WIDTH
    )
    query_heads = query_matrix.reshape(row_count, kv_heads, query_group_width, HEAD_WIDTH)
    scores = (
        jnp.einsum("tkgd,skd->kgts", query_heads, near_keys, preferred_element_type=jnp.float32)
        * scale_factor
    )
    offsets = (
        jnp.arange(row_count, dtype=jnp.int32)[:, None]
        + row_count
        - jnp.arange(2 * row_count, dtype=jnp.int32)[None, :]
    )
    key_pos = seq_rank * row_count - row_count + jnp.arange(2 * row_count, dtype=jnp.int32)
    window_bounds = window.reshape(kv_heads, query_group_width)
    allowed = (
        (offsets >= 0)[None, None]
        & (offsets[None, None] < window_bounds[:, :, None, None])
        & (key_pos >= 0)[None, None, None, :]
    )
    probs = softmax_rows(scores, allowed)
    context = jnp.einsum("kgts,skd->tkgd", probs, near_values, preferred_element_type=jnp.float32)
    context = context.astype(jnp.bfloat16).reshape(row_count, query_columns)
    stream = add_branch(tokens, jnp.dot(context, self_output, preferred_element_type=jnp.float32))
    cache_in = normed_full(stream, norm_gains[1])
    cached_key_rows = project(cache_in, shared_key_value[0])
    cached_value_rows = project(cache_in, shared_key_value[1])
    all_keys, all_values = (
        lax.all_gather(cached_key_rows, "seq", axis=0, tiled=True),
        lax.all_gather(cached_value_rows, "seq", axis=0, tiled=True),
    )
    key_lookup_matrix = all_keys.reshape(-1, KEY_BLOCK_TOKENS, kv_columns)
    value_lookup_matrix = all_values.reshape(-1, KEY_BLOCK_TOKENS, kv_columns)
    query_weights, output_weights = (
        lax.all_gather(cross_query, "seq", axis=1, tiled=True),
        lax.all_gather(cross_output, "seq", axis=2, tiled=True),
    )
    query_blocks = row_count // KEY_BLOCK_TOKENS
    inner = jnp.arange(KEY_BLOCK_TOKENS, dtype=jnp.int32)
    block_ids = seq_rank * query_blocks + jnp.arange(query_blocks, dtype=jnp.int32)
    query_pos = block_ids[:, None] * KEY_BLOCK_TOKENS + inner[None, :]
    for section in range(SECTIONS):
        section_in = normed_full(stream, norm_gains[2 + section])
        query_matrix = project(section_in, query_weights[section])
        lists = key_blocks[section]
        clamped_index = jnp.maximum(lists, 0)
        picked_keys = jnp.take(key_lookup_matrix, clamped_index.reshape(-1), axis=0).reshape(
            query_blocks, LISTED_BLOCKS * KEY_BLOCK_TOKENS, kv_heads, HEAD_WIDTH
        )
        picked_values = jnp.take(value_lookup_matrix, clamped_index.reshape(-1), axis=0).reshape(
            query_blocks, LISTED_BLOCKS * KEY_BLOCK_TOKENS, kv_heads, HEAD_WIDTH
        )
        query_heads = query_matrix.reshape(
            query_blocks, KEY_BLOCK_TOKENS, kv_heads, query_group_width, HEAD_WIDTH
        )
        scores = (
            jnp.einsum(
                "btkgd,bskd->bkgts", query_heads, picked_keys, preferred_element_type=jnp.float32
            )
            * scale_factor
        )
        listed_pos = (clamped_index[:, :, None] * KEY_BLOCK_TOKENS + inner[None, None, :]).reshape(
            query_blocks, LISTED_BLOCKS * KEY_BLOCK_TOKENS
        )
        present = jnp.repeat(lists >= 0, KEY_BLOCK_TOKENS, axis=1)
        allowed = present[:, None, :] & (listed_pos[:, None, :] <= query_pos[:, :, None])
        probs = softmax_rows(scores, allowed[:, None, None])
        context = jnp.einsum(
            "bkgts,bskd->btkgd", probs, picked_values, preferred_element_type=jnp.float32
        )
        context = context.astype(jnp.bfloat16).reshape(row_count, query_columns)
        partial_value = jnp.dot(
            context, output_weights[section], preferred_element_type=jnp.float32
        )
        stream = add_branch(stream, partial_value)
    return stream


def solution(mesh):
    placed = (
        P("seq", "head"),
        P(),
        P("head"),
        P(None, "head"),
        P(None, None, "head"),
        P("head", None),
        P(None, None, "head"),
        P(None, "seq", "head"),
        P(None, "head", "seq"),
        P(None, "seq", None),
    )
    return jax.shard_map(
        body, mesh=mesh, in_specs=placed, out_specs=P("seq", "head"), check_vma=False
    )
```

profile of v0, /device:TPU:0, one launch (start us, length us, event | category | flops | bytes accessed | tf_op | source)
XLA Modules:
  0.0 607.8 jit_solution(6547917369271950071)
XLA Ops:
  6.5 13.0 %all_gather.25 = bf16[128,3072]{1,0:T(8,128)(2,1)S(1)} all-gather(bf16[128,1536]{1,0:T(8,128)(2,1)} %param.12), channel_id=1, replica_groups=mesh['seq'=16,'head'=2] {'head'}, dimensions={1}, use_global_device_ids=true | all-gather | bytes 1179648 | tf_op jit(solution)/shard_map/all_gather | solution.py:50
  19.5 1.9 fusion.120
  21.4 0.2 fusion.51
  21.6 2.7 fusion.77
  24.4 1.6 collective-permute-start
  26.0 2.5 fusion.80
  28.5 4.3 collective-permute-start.1
  32.8 1.5 convolution_convert_fusion.1
  35.0 0.8 fusion.121
  35.8 0.3 convolution_convert_fusion.2
  36.2 6.0 convolution_convert_fusion
  42.3 19.5 %reduce-scatter.5.cloned.1.call-done = bf16[128,1536]{1,0:T(8,128)(2,1)} async-done(((bf16[128,3072]{1,0:T(8,128)(2,1)}), bf16[128,1536]{1,0:T(8,128)(2,1)}) %reduce-scatter.5.cloned.1.call-update) | async-done | bytes 393232 | tf_op jit(solution)/shard_map/reduce_scatter | solution.py:57
  61.7 1.1 fusion.98
  62.8 11.5 %all_gather.26 = bf16[128,3072]{1,0:T(8,128)(2,1)S(1)} all-gather(bf16[128,1536]{1,0:T(8,128)(2,1)S(1)} %fusion.98), channel_id=1, replica_groups=mesh['seq'=16,'head'=2] {'head'}, dimensions={1}, use_global_device_ids=true | all-gather | bytes 1179648 | tf_op jit(solution)/shard_map/all_gather | solution.py:50
  74.3 0.2 fusion.54
  74.6 3.2 fusion.83
  77.9 3.2 fusion.86
  81.1 0.5 all-gather.9.cloned.1.call-update
  81.7 0.5 all-gather.11.cloned.1.call-update
  82.3 0.6 compare_and_fusion.3
  83.3 4.0 compare_and_fusion
  87.3 32.0 %all-gather.5.cloned.1.call-done = bf16[2048,512]{1,0:T(8,128)(2,1)} async-done(((bf16[128,512]{1,0:T(8,128)(2,1)}), bf16[2048,512]{1,0:T(8,128)(2,1)}) %all-gather.5.cloned.1.call-update) | async-done | bytes 2097168 | tf_op jit(solution)/shard_map/all_gather | solution.py:102
  119.3 2.3 gather_fusion
  121.6 40.3 %all-gather.7.cloned.1.call-done = bf16[2048,512]{1,0:T(8,128)(2,1)} async-done(((bf16[128,512]{1,0:T(8,128)(2,1)}), bf16[2048,512]{1,0:T(8,128)(2,1)}) %all-gather.7.cloned.1.call-update) | async-done | bytes 2097168 | tf_op jit(solution)/shard_map/all_gather | solution.py:101
  161.9 3.6 gather_fusion.1
  165.5 4.5 broadcast_select_fusion.5
  170.1 4.1 reshape.657
  174.2 2.2 reshape.656
  176.4 129.2 %all-gather.9.cloned.1.call-done = bf16[3,3072,1536]{2,1,0:T(8,128)(2,1)} async-done(((bf16[3,192,1536]{2,1,0:T(8,128)(2,1)}), bf16[3,3072,1536]{2,1,0:T(8,128)(2,1)}) %all-gather.9.cloned.1.call-update) | async-done | bytes 28311568 | tf_op jit(solution)/shard_map/all_gather | solution.py:107
  305.6 6.0 fusion.34
  311.6 1.2 copy.51
  312.9 3.2 fusion.4
  316.1 2.6 fusion.1
  318.7 3.8 fusion.62
  322.5 127.9 %all-gather.11.cloned.1.call-done = bf16[3,1536,3072]{1,2,0:T(8,128)(2,1)} async-done(((bf16[3,1536,192]{1,2,0:T(8,128)(2,1)}), bf16[3,1536,3072]{1,2,0:T(8,128)(2,1)}) %all-gather.11.cloned.1.call-update) | async-done | bytes 28311568 | tf_op jit(solution)/shard_map/all_gather | solution.py:108
  450.5 7.9 %fusion.19 = bf16[128,3072]{1,0:T(8,128)(2,1)} fusion(bf16[128,1536]{0,1:T(8,128)(2,1)S(1)} %bitcast.231, bf16[3,1536,3072]{1,2,0:T(8,128)(2,1)} %all-gather.11.cloned.1.call-done), kind=kOutput, calls=%fused_computation.40 | convolution fusion | flops 1208352768 | bytes 10616832 | tf_op jit(solution)/shard_map/dot_general | solution.py:144
  458.5 2.0 gather_fusion.4
  460.5 3.6 gather_fusion.5
  464.1 3.7 gather_fusion.3
  467.8 2.0 gather_fusion.2
  469.8 5.6 broadcast_select_fusion.1
  475.5 4.0 reshape.659
  479.5 4.0 reshape.658
  483.5 1.1 fusion.103
  484.7 12.3 %all_gather.31 = bf16[128,3072]{1,0:T(8,128)(2,1)S(1)} all-gather(bf16[128,1536]{1,0:T(8,128)(2,1)S(1)} %fusion.103), channel_id=1, replica_groups=mesh['seq'=16,'head'=2] {'head'}, dimensions={1}, use_global_device_ids=true | all-gather | bytes 1179648 | tf_op jit(solution)/shard_map/all_gather | solution.py:50
  497.2 5.9 fusion.35
  503.2 1.9 copy.57
  505.1 3.8 fusion.5
  508.8 2.6 fusion.2
  511.4 5.4 fusion.67
  516.8 7.8 %fusion.20 = bf16[128,3072]{1,0:T(8,128)(2,1)} fusion(bf16[128,1536]{0,1:T(8,128)(2,1)S(1)} %bitcast.233, bf16[3,1536,3072]{1,2,0:T(8,128)(2,1)} %all-gather.11.cloned.1.call-done), kind=kOutput, calls=%fused_computation.41 | convolution fusion | flops 1208352768 | bytes 10616832 | tf_op jit(solution)/shard_map/dot_general | solution.py:144
  524.8 4.0 reshape.661
  528.8 2.1 reshape.660
  530.9 11.6 %reduce-scatter.9.cloned.1.call-done = bf16[128,1536]{1,0:T(8,128)(2,1)} async-done(((bf16[128,3072]{1,0:T(8,128)(2,1)}), bf16[128,1536]{1,0:T(8,128)(2,1)}) %reduce-scatter.9.cloned.1.call-update) | async-done | bytes 393232 | tf_op jit(solution)/shard_map/reduce_scatter | solution.py:57
  542.5 1.2 fusion.99
  543.7 11.7 %all_gather.32 = bf16[128,3072]{1,0:T(8,128)(2,1)S(1)} all-gather(bf16[128,1536]{1,0:T(8,128)(2,1)S(1)} %fusion.99), channel_id=1, replica_groups=mesh['seq'=16,'head'=2] {'head'}, dimensions={1}, use_global_device_ids=true | all-gather | bytes 1179648 | tf_op jit(solution)/shard_map/all_gather | solution.py:50
  555.7 6.0 fusion.36
  561.7 1.9 copy.63
  563.6 3.1 fusion.6
  566.8 2.6 fusion.3
  569.3 3.9 fusion.72
  573.2 7.9 %fusion.21 = bf16[128,3072]{1,0:T(8,128)(2,1)} fusion(bf16[128,1536]{0,1:T(8,128)(2,1)S(1)} %bitcast.232, bf16[3,1536,3072]{1,2,0:T(8,128)(2,1)} %all-gather.11.cloned.1.call-done), kind=kOutput, calls=%fused_computation.42 | convolution fusion | flops 1208352768 | bytes 10616832 | tf_op jit(solution)/shard_map/dot_general | solution.py:144
  581.1 17.6 %reduce-scatter.11.cloned.1.call-done = bf16[128,1536]{1,0:T(8,128)(2,1)} async-done(((bf16[128,3072]{1,0:T(8,128)(2,1)}), bf16[128,1536]{1,0:T(8,128)(2,1)}) %reduce-scatter.11.cloned.1.call-update) | async-done | bytes 393232 | tf_op jit(solution)/shard_map/reduce_scatter | solution.py:57
  598.7 2.1 convert_add_fusion
  (90 shorter events, 2.0 us)
Async XLA Ops:
  6.5 55.2 %reduce-scatter.5.cloned.1.call-start = ((), (), s32[]{:S(2)}) async-start(), calls=%async_computation.4 | async-start | bytes 1179648 | tf_op jit(solution)/shard_map/reduce_scatter | solution.py:57
  21.6 11.2 %copy-start = (bf16[3072,1536]{1,0:T(8,128)(2,1)S(1)}, bf16[3072,1536]{1,0:T(8,128)(2,1)}, u32[]{:S(2)}) copy-start(bf16[3072,1536]{1,0:T(8,128)(2,1)} %param.15) | copy-start | bytes 28311556
  24.4 10.4 %collective-permute-start = (bf16[128,512]{1,0:T(8,128)(2,1)S(1)}, bf16[128,512]{1,0:T(8,128)(2,1)S(1)}, u32[]{:S(2)}, u32[]{:S(2)}) collective-permute-start(bf16[128,512]{1,0:T(8,128)(2,1)S(1)} %fusion.77), channel_id=1, source_target_pairs={{0,2},{2,4},{4,6},{6,8},{8,10},{10,12},{12,14},{14,16},{16,18},{18... | collective-permute-start | bytes 393224 | tf_op jit(solution)/shard_map/ppermute | solution.py:19
  28.5 6.4 %collective-permute-start.1 = (bf16[128,512]{1,0:T(8,128)(2,1)S(1)}, bf16[128,512]{1,0:T(8,128)(2,1)S(1)}, u32[]{:S(2)}, u32[]{:S(2)}) collective-permute-start(bf16[128,512]{1,0:T(8,128)(2,1)S(1)} %fusion.80), channel_id=1, source_target_pairs={{0,2},{2,4},{4,6},{6,8},{8,10},{10,12},{12,14},{14,16},{16,18},{18... | collective-permute-start | bytes 393224 | tf_op jit(solution)/shard_map/ppermute | solution.py:19
  32.8 1.8 copy-start.19
  36.1 25.6 %copy-start.2 = (bf16[128,1536]{1,0:T(8,128)(2,1)S(1)}, bf16[128,1536]{1,0:T(8,128)(2,1)}, u32[]{:S(2)}) copy-start(bf16[128,1536]{1,0:T(8,128)(2,1)} %param.12) | copy-start | bytes 1179652
  42.2 77.1 %all-gather.5.cloned.1.call-start = ((), (), s32[]{:S(2)}) async-start(), calls=%async_computation.5 | async-start | bytes 2228224 | tf_op jit(solution)/shard_map/all_gather | solution.py:102
  74.6 3.3 copy-start.20
  77.8 84.1 %all-gather.7.cloned.1.call-start = ((), (), s32[]{:S(2)}) async-start(), calls=%async_computation.6 | async-start | bytes 2228224 | tf_op jit(solution)/shard_map/all_gather | solution.py:101
  81.0 1.3 copy-start.13
  81.1 224.5 %all-gather.9.cloned.1.call-start = ((), (), s32[]{:S(2)}) async-start(), calls=%async_computation.7 | async-start | bytes 30081024 | tf_op jit(solution)/shard_map/all_gather | solution.py:107
  81.6 368.8 %all-gather.11.cloned.1.call-start = ((), (), s32[]{:S(2)}) async-start(), calls=%async_computation.8 | async-start | bytes 30081024 | tf_op jit(solution)/shard_map/all_gather | solution.py:108
  82.2 401.3 %reduce-scatter.7.cloned.1.call-start = ((), (), s32[]{:S(2)}) async-start(), calls=%async_computation.9 | async-start | bytes 1179648 | tf_op jit(solution)/shard_map/reduce_scatter | solution.py:57
  170.1 4.1 copy-start.3
  174.2 131.4 %copy-start.21 = (f32[128]{0:T(128)S(1)}, f32[128]{0:T(128)}, u32[]{:S(2)}) copy-start(f32[128]{0:T(128)} %copy-done.20) | copy-start | bytes 1540
  305.6 7.3 %copy-start.9 = (bf16[2048,4,128]{2,1,0:T(4,128)(2,1)S(1)}, bf16[2048,4,128]{2,1,0:T(4,128)(2,1)}, u32[]{:S(2)}) copy-start(bf16[2048,4,128]{2,1,0:T(4,128)(2,1)} %reshape.657) | copy-start | bytes 6291460
  312.9 3.2 copy-start.12
  316.1 2.6 copy-start.8
  450.5 8.0 %copy-start.18 = (s32[16]{0:T(128)S(1)}, s32[16]{0:T(128)}, u32[]{:S(2)}) copy-start(s32[16]{0:T(128)} %get-tuple-element.7) | copy-start | bytes 196
  450.5 8.0 %copy-start.17 = (s32[16]{0:T(128)S(1)}, s32[16]{0:T(128)}, u32[]{:S(2)}) copy-start(s32[16]{0:T(128)} %get-tuple-element.26) | copy-start | bytes 196
  450.5 8.0 %copy-start.1 = (bf16[2048,512]{1,0:T(8,128)(2,1)S(1)}, bf16[2048,512]{1,0:T(8,128)(2,1)}, u32[]{:S(2)}) copy-start(bf16[2048,512]{1,0:T(8,128)(2,1)} %all-gather.5.cloned.1.call-done) | copy-start | bytes 6291460
  458.4 84.1 %reduce-scatter.9.cloned.1.call-start = ((), (), s32[]{:S(2)}) async-start(), calls=%async_computation.10 | async-start | bytes 1179648 | tf_op jit(solution)/shard_map/reduce_scatter | solution.py:57
  467.8 2.0 copy-start.15
  467.8 2.0 copy-start.16
  479.5 4.0 copy-start.4
  483.5 13.7 %copy-start.14 = (f32[1,3072]{1,0:T(1,128)S(1)}, f32[1,3072]{1,0:T(1,128)}, u32[]{:S(2)}) copy-start(f32[1,3072]{1,0:T(1,128)} %get-tuple-element.16) | copy-start | bytes 36868
  497.2 7.9 %copy-start.11 = (pred[128,2048]{0,1:T(8,128)(4,1)S(1)}, pred[128,2048]{0,1:T(8,128)(4,1)}, u32[]{:S(2)}) copy-start(pred[128,2048]{0,1:T(8,128)(4,1)} %get-tuple-element.30) | copy-start | bytes 786436
  524.7 74.0 %reduce-scatter.11.cloned.1.call-start = ((), (), s32[]{:S(2)}) async-start(), calls=%async_computation.11 | async-start | bytes 1179648 | tf_op jit(solution)/shard_map/reduce_scatter | solution.py:57
  528.8 13.7 %copy-start.5 = (bf16[128,1536]{1,0:T(8,128)(2,1)S(1)}, bf16[128,1536]{1,0:T(8,128)(2,1)}, u32[]{:S(2)}) copy-start(bf16[128,1536]{1,0:T(8,128)(2,1)} %reduce-scatter.7.cloned.1.call-done) | copy-start | bytes 1179652
  555.7 8.0 %copy-start.7 = (bf16[2048,4,128]{2,1,0:T(4,128)(2,1)S(1)}, bf16[2048,4,128]{2,1,0:T(4,128)(2,1)}, u32[]{:S(2)}) copy-start(bf16[2048,4,128]{2,1,0:T(4,128)(2,1)} %reshape.661) | copy-start | bytes 6291460
  566.7 2.6 copy-start.6
  573.2 25.5 %copy-start.10 = (bf16[128,1536]{1,0:T(8,128)(2,1)S(1)}, bf16[128,1536]{1,0:T(8,128)(2,1)}, u32[]{:S(2)}) copy-start(bf16[128,1536]{1,0:T(8,128)(2,1)} %reduce-scatter.9.cloned.1.call-done) | copy-start | bytes 1179652
Sparse Core Ops, SparseCore 0:
  42.3 19.3 reduce-scatter.4
  77.9 41.3 all-gather.4
  121.7 40.1 all-gather.6
  163.4 142.1 all-gather.8
  307.1 143.3 all-gather.10
  458.5 17.4 reduce-scatter.6
  524.8 17.6 reduce-scatter.8
  581.2 17.4 reduce-scatter.10
where the time goes:
time: 615 us; the launch traced here: 608 us
  waiting for transfers between devices  379 us (62%)
  matrix products  85.1 us (14%)
  blocking collectives  48.5 us (8%)
  local copies, waits for them, and re-layouts  45.5 us (7%)
  other arithmetic  29.1 us (5%)
  between operations  14.1 us (2%)
  starting transfers between devices  6.16 us (1%)
    all_gather x1, waiting for transfers between devices, body(): lax.all_gather(cross_query, 'seq', axis=1, tiled=True)  129 us
    all_gather x1, waiting for transfers between devices, body(): lax.all_gather(cross_output, 'seq', axis=2, tiled=True)  128 us
    reduce_scatter x4, waiting for transfers between devices, add_branch(): lax.psum_scatter(partial_value.astype(jnp.bfloat16), 'head', scatter_dime...  48.7 us
    all_gather x4, blocking collectives, normed_full(): lax.all_gather(stream.astype(jnp.float32).astype(jnp.bfloat16), 'head', a...  48.5 us
    all_gather x1, waiting for transfers between devices, body(): lax.all_gather(cached_key_rows, 'seq', axis=0, tiled=True)  40.3 us
    all_gather x1, waiting for transfers between devices, body(): lax.all_gather(cached_value_rows, 'seq', axis=0, tiled=True)  32 us
    dot_general x8, matrix products, project(): jnp.dot(inputs, weight, preferred_element_type=jnp.float32)  31.1 us
    dot_general x3, matrix products, body(): jnp.dot(context, output_weights[section], preferred_element_type=jnp.floa...  23.6 us
  transfers between devices with their start and end apart: 10, of which 7 were waited for; matrix products, arithmetic and copies ran while one was open for 13% of the time, Pallas kernels for 0%

commit v1 on v0

v1 whole, which is shorter than its diff:
```python
import functools

import jax
import jax.numpy as jnp
import numpy as np
from jax import lax
from jax.experimental import pallas as pl
from jax.experimental.pallas import tpu as pltpu
from jax.sharding import PartitionSpec as P

HEAD_WIDTH = 128
EPSILON = 1e-06
MASKED = -1e30
CORES = 2


def dot(a, b, contract):
    return lax.dot_general(a, b, ((contract[0], contract[1]), ((), ())), preferred_element_type=jnp.float32)


def listed_kernel(group, lists_ref, q_ref, k_ref, v_ref, o_ref, kg, vg):
    rows = q_ref.shape[0]
    slots = lists_ref.shape[0]
    width = HEAD_WIDTH
    per = 4 if slots % 4 == 0 else 1
    factor = HEAD_WIDTH ** (-0.5) * 1.4426950408889634
    for slot in range(slots):
        at = jnp.maximum(lists_ref[slot], 0) * rows
        at = pl.multiple_of(at, rows)
        kg[slot * rows : (slot + 1) * rows, :] = k_ref[pl.ds(at, rows), :]
        vg[slot * rows : (slot + 1) * rows, :] = v_ref[pl.ds(at, rows), :]
    q = jnp.concatenate([q_ref[:, g * width : (g + 1) * width] for g in range(group)], axis=0)
    own_row = lax.broadcasted_iota(jnp.int32, (rows, rows), 0)
    own_col = lax.broadcasted_iota(jnp.int32, (rows, rows), 1)
    causal = jnp.concatenate([own_col <= own_row] * group, axis=0)
    parts = []
    for start in range(0, slots, per):
        s = dot(q, kg[start * rows : (start + per) * rows, :], ((1,), (1,)))
        pieces = []
        for i in range(per):
            piece = s[:, i * rows : (i + 1) * rows]
            if start + i == 0:
                piece = jnp.where(causal, piece, MASKED)
            else:
                piece = jnp.where(lists_ref[start + i] >= 0, piece, MASKED)
            pieces.append(piece)
        parts.append(jnp.concatenate(pieces, axis=1))
    largest = functools.reduce(jnp.maximum, [jnp.max(p, axis=1, keepdims=True) for p in parts])
    total = jnp.zeros_like(largest)
    acc = jnp.zeros((group * rows, width), jnp.float32)
    for n, p in enumerate(parts):
        weights = jnp.exp2((p - largest) * factor)
        total = total + jnp.sum(weights, axis=1, keepdims=True)
        at = n * per * rows
        acc = acc + dot(weights.astype(jnp.bfloat16), vg[at : at + per * rows, :], ((1,), (0,)))
    acc = acc / total
    for g in range(group):
        o_ref[:, g * width : (g + 1) * width] = acc[g * rows : (g + 1) * rows].astype(o_ref.dtype)


def listed_attention(lists, query, cache, kv_heads):
    rows, columns = query.shape
    keys = cache.shape[0]
    group = columns // (kv_heads * HEAD_WIDTH)
    slots = lists.shape[0]
    spec = pltpu.PrefetchScalarGridSpec(
        num_scalar_prefetch=1,
        grid=(kv_heads,),
        in_specs=[
            pl.BlockSpec((rows, group * HEAD_WIDTH), lambda h, _: (0, h)),
            pl.BlockSpec((keys, HEAD_WIDTH), lambda h, _: (0, h)),
            pl.BlockSpec((keys, HEAD_WIDTH), lambda h, _: (0, kv_heads + h)),
        ],
        out_specs=pl.BlockSpec((rows, group * HEAD_WIDTH), lambda h, _: (0, h)),
        scratch_shapes=[pltpu.VMEM((slots * rows, HEAD_WIDTH), jnp.bfloat16)] * 2,
    )
    return pl.pallas_call(
        functools.partial(listed_kernel, group),
        grid_spec=spec,
        out_shape=jax.ShapeDtypeStruct((rows, columns), jnp.bfloat16),
        compiler_params=pltpu.CompilerParams(vmem_limit_bytes=40 << 20),
        cost_estimate=pl.CostEstimate(
            flops=4 * rows * columns * slots * rows,
            bytes_accessed=2 * cache.size + 4 * query.size,
            transcendentals=rows * slots * rows * columns // HEAD_WIDTH,
        ),
        name="listed_attention",
    )(lists, query, cache, cache)


def query_kernel(count, x_ref, *refs):
    w_refs, o_ref = refs[:count], refs[count]
    piece = x_ref.shape[0] // count
    acc = None
    for j in range(count):
        left = x_ref[j * piece : (j + 1) * piece, :].astype(jnp.float32).T.astype(jnp.bfloat16)
        term = dot(left, w_refs[j][...], ((1,), (0,)))
        acc = term if acc is None else acc + term
    o_ref[...] = acc


def query_project(scaled, pieces):
    columns = pieces[0].shape[1]
    tokens = scaled.shape[1]
    tile = columns // 3
    return pl.pallas_call(
        functools.partial(query_kernel, len(pieces)),
        grid=(columns // tile,),
        in_specs=[pl.BlockSpec(scaled.shape, lambda n: (0, 0))]
        + [pl.BlockSpec((p.shape[0], tile), lambda n: (0, n)) for p in pieces],
        out_specs=pl.BlockSpec((tokens, tile), lambda n: (0, n)),
        out_shape=jax.ShapeDtypeStruct((tokens, columns), jnp.float32),
        compiler_params=pltpu.CompilerParams(vmem_limit_bytes=40 << 20),
        cost_estimate=pl.CostEstimate(
            flops=2 * tokens * columns * scaled.shape[0],
            bytes_accessed=2 * columns * scaled.shape[0] + 4 * tokens * columns,
            transcendentals=0,
        ),
        name="query_project",
    )(scaled, *pieces)


def output_kernel(count, own_ref, other_ref, *refs):
    w_refs, o_ref = refs[:count], refs[count]
    piece = w_refs[0].shape[0]
    context = jnp.concatenate([own_ref[...], other_ref[...]], axis=0)
    for j in range(count):
        term = dot(w_refs[j][...], context, ((1,), (1,)))
        o_ref[j * piece : (j + 1) * piece, :] = term.astype(o_ref.dtype)


def output_project(own, other, pieces):
    features = sum(p.shape[0] for p in pieces)
    tokens = own.shape[0] + other.shape[0]
    return pl.pallas_call(
        functools.partial(output_kernel, len(pieces)),
        out_shape=jax.ShapeDtypeStruct((features, tokens), jnp.bfloat16),
        compiler_params=pltpu.CompilerParams(vmem_limit_bytes=40 << 20),
        cost_estimate=pl.CostEstimate(
            flops=2 * tokens * features * own.shape[1],
            bytes_accessed=2 * features * own.shape[1] + 2 * tokens * features,
            transcendentals=0,
        ),
        name="output_project",
    )(own, other, *pieces)


def body(
    tokens,
    norm_gains,
    window,
    self_query,
    self_key_value,
    self_output,
    shared_key_value,
    cross_query,
    cross_output,
    key_blocks,
):
    seq_count = lax.axis_size("seq")
    head_count = lax.axis_size("head")
    seq_rank = lax.axis_index("seq")
    head_rank = lax.axis_index("head")
    rows = tokens.shape[0]
    model_width = self_query.shape[0]
    kv_columns = self_key_value.shape[2]
    query_columns = self_query.shape[1]
    kv_heads = kv_columns // HEAD_WIDTH
    group = query_columns // kv_columns
    sections = cross_query.shape[0]
    shard = cross_query.shape[1]
    chips = seq_count // CORES
    scale_factor = HEAD_WIDTH ** (-0.5)

    order = list(range(0, chips, 2)) + list(range(1, chips, 2))[::-1]
    place = np.argsort(np.array(order))
    rightward, leftward = [], []
    for core in range(CORES):
        ranks = [chip * CORES + core for chip in order]
        rightward += [(ranks[i], ranks[(i + 1) % chips]) for i in range(chips)]
        leftward += [(ranks[i], ranks[i - 1]) for i in range(chips)]
    twins = [(rank, rank ^ 1) for rank in range(seq_count)]

    my_core = seq_rank % CORES
    my_place = jnp.take(jnp.asarray(place, jnp.int32), seq_rank // CORES)
    ring_chips = jnp.take(jnp.asarray(order, jnp.int32), (my_place + jnp.arange(chips)) % chips)
    own_shards = ring_chips * CORES + my_core
    twin_shards = ring_chips * CORES + (1 - my_core)

    def to_twin(value):
        return lax.ppermute(value, "seq", twins)

    def head_shift(value, k):
        return lax.ppermute(value, "head", [(i, (i + k) % head_count) for i in range(head_count)])

    def over_heads(partial):
        total = partial.astype(jnp.float32)
        for k in range(1, head_count):
            total = total + head_shift(partial, k).astype(jnp.float32)
        return total

    def ring(value, more_right, after):
        pieces = {0: value}
        right = chips // 2 if more_right else chips - 1 - chips // 2
        left = chips - 1 - right
        if after is not None:
            value, _ = lax.optimization_barrier((value, after))
        moving = value
        marks = []
        to_right, to_left = value, value
        for step in range(max(right, left)):
            if step < right:
                to_right = lax.ppermute(to_right, "seq", rightward)
                pieces[-(step + 1) % chips] = to_right
            if step < left:
                to_left = lax.ppermute(to_left, "seq", leftward)
                pieces[step + 1] = to_left
            marks.append((to_right, to_left))
        return [pieces[j] for j in range(chips)], marks

    shards = []
    for s in range(sections):
        shards += [cross_query[s], cross_output[s].T]
    gathered = []
    marks = None
    for m, value in enumerate(shards):
        after = None
        if marks is not None:
            after = marks[0 if m == 1 else 1]
        pieces, marks = ring(value, m % 2 == 0, after)
        gathered.append(pieces)

    parts = [tokens] + [head_shift(tokens, k) for k in range(1, head_count)]
    parts = jnp.stack(parts)
    sources = (head_rank - jnp.arange(head_count)) % head_count
    back = jnp.zeros((head_count,), jnp.int32).at[sources].set(jnp.arange(head_count, dtype=jnp.int32))
    full = jnp.take(parts, back, axis=0).transpose(1, 0, 2).reshape(rows, model_width).astype(jnp.float32)

    def normed(values, gain_row):
        factor = lax.rsqrt(jnp.mean(values * values, axis=1, keepdims=True) + EPSILON)
        return (values * factor * gain_row[None, :]).astype(jnp.bfloat16)

    def project(inputs, weight):
        return jnp.dot(inputs, weight, preferred_element_type=jnp.float32).astype(jnp.bfloat16)

    first = normed(full, norm_gains[0])
    keys_own = project(first, self_key_value[0])
    values_own = project(first, self_key_value[1])
    along = [(i, i + 1) for i in range(seq_count - 1)]
    keys_prev = lax.ppermute(keys_own, "seq", along)
    values_prev = lax.ppermute(values_own, "seq", along)
    query_matrix = project(first, self_query)
    near_keys = jnp.concatenate([keys_prev, keys_own], axis=0).reshape(2 * rows, kv_heads, HEAD_WIDTH)
    near_values = jnp.concatenate([values_prev, values_own], axis=0).reshape(2 * rows, kv_heads, HEAD_WIDTH)
    query_heads = query_matrix.reshape(rows, kv_heads, group, HEAD_WIDTH)
    scores = jnp.einsum("tkgd,skd->kgts", query_heads, near_keys, preferred_element_type=jnp.float32) * scale_factor
    offsets = jnp.arange(rows, dtype=jnp.int32)[:, None] + rows - jnp.arange(2 * rows, dtype=jnp.int32)[None, :]
    key_pos = seq_rank * rows - rows + jnp.arange(2 * rows, dtype=jnp.int32)
    bounds = window.reshape(kv_heads, group)
    allowed = (
        (offsets >= 0)[None, None]
        & (offsets[None, None] < bounds[:, :, None, None])
        & (key_pos >= 0)[None, None, None, :]
    )
    scores = jnp.where(allowed, scores, MASKED)
    weights = jnp.exp(scores - jnp.max(scores, axis=-1, keepdims=True))
    probs = (weights / jnp.sum(weights, axis=-1, keepdims=True)).astype(jnp.bfloat16)
    context = jnp.einsum("kgts,skd->tkgd", probs, near_values, preferred_element_type=jnp.float32)
    context = context.astype(jnp.bfloat16).reshape(rows, query_columns)
    partial = jnp.dot(context, self_output, preferred_element_type=jnp.float32).astype(jnp.bfloat16)
    stream = full + over_heads(partial)

    cache_in = normed(stream, norm_gains[1])
    own_cache = jnp.concatenate(
        [project(cache_in, shared_key_value[0]), project(cache_in, shared_key_value[1])], axis=1
    )
    cache = lax.all_gather(own_cache, "seq", axis=0, tiled=True)

    by_shard = stream.T.reshape(seq_count, shard, rows)
    mine = jnp.take(by_shard, own_shards, axis=0)
    others = to_twin(jnp.take(by_shard, twin_shards, axis=0))
    state = jnp.concatenate([mine, others], axis=2).reshape(chips * shard, CORES * rows)
    gains = jnp.take(norm_gains.reshape(-1, seq_count, shard), own_shards, axis=1).reshape(-1, chips * shard)

    for s in range(sections):
        query_pieces, output_pieces = gathered[2 * s], gathered[2 * s + 1]
        scaled = (state * gains[2 + s][:, None]).astype(jnp.bfloat16)
        squares = jnp.sum(state * state, axis=0)
        partial_query = query_project(scaled, query_pieces)
        from_twin = to_twin(partial_query[rows:].astype(jnp.bfloat16)).astype(jnp.float32)
        squares = squares[:rows] + to_twin(squares[rows:])
        factor = lax.rsqrt(squares / model_width + EPSILON)
        query = ((partial_query[:rows] + from_twin) * factor[:, None]).astype(jnp.bfloat16)
        own = listed_attention(key_blocks[s, 0], query, cache, kv_heads)
        other = to_twin(own)
        partial = output_project(own, other, output_pieces)
        if s < sections - 1:
            state = state + over_heads(partial)

    share = chips // head_count
    per_head = seq_count // head_count

    def of_head(head, value):
        at = jnp.nonzero(own_shards // per_head == head, size=share)[0]
        return jnp.take(value.reshape(chips, shard, CORES * rows), at, axis=0)

    total = of_head(head_rank, partial).astype(jnp.float32)
    for k in range(1, head_count):
        total = total + head_shift(of_head((head_rank + k) % head_count, partial), k).astype(jnp.float32)
    total = of_head(head_rank, state) + total
    kept = total[:, :, :rows]
    brought = to_twin(total[:, :, rows:])
    own_ids = jnp.take(own_shards, jnp.nonzero(own_shards // per_head == head_rank, size=share)[0])
    twin_ids = own_ids + 1 - 2 * my_core
    ids = jnp.concatenate([own_ids, twin_ids]) - head_rank * per_head
    back = jnp.argsort(ids)
    result = jnp.take(jnp.concatenate([kept, brought], axis=0), back, axis=0)
    return result.reshape(per_head * shard, rows).T


def solution(mesh):
    placed = (
        P("seq", "head"),
        P(),
        P("head"),
        P(None, "head"),
        P(None, None, "head"),
        P("head", None),
        P(None, None, "head"),
        P(None, "seq", "head"),
        P(None, "head", "seq"),
        P(None, "seq", None),
    )
    return jax.shard_map(body, mesh=mesh, in_specs=placed, out_specs=P("seq", "head"), check_vma=False)
```

time: 615 us -> 416 us (0.68); the launches traced: 608 us -> 415 us
  waiting for transfers between devices: 379 us -> 204 us
  matrix products: 85.1 us -> 17.4 us
  Pallas kernels: 0 us -> 58.4 us
  starting transfers between devices: 6.16 us -> 62 us
  blocking collectives: 48.5 us -> 0 us
  local copies, waits for them, and re-layouts: 45.5 us -> 34.8 us
  other arithmetic: 29.1 us -> 22.9 us
    all_gather x4 -> x1, waiting for transfers between devices: 329 us -> 0.02 us  [body(): cache = lax.all_gather(own_cache, 'seq', axis=0, tiled=True)]
    ppermute x2 -> x60, waiting for transfers between devices: 0.01 us -> 204 us  [the longest x21 110 us: ring(): to_right = lax.ppermute(to_right, 'seq', rightward)]
    pallas_call x0 -> x9, Pallas kernels: none -> 58.4 us  [the longest x3 32.2 us: listed_attention(): pl.pallas_call(functools.partial(listed_kernel, group), grid_spec=spec, o...]
    ppermute x2 -> x60, starting transfers between devices: 5.87 us -> 62 us  [the longest x21 28.7 us: ring(): to_left = lax.ppermute(to_left, 'seq', leftward)]
    reduce_scatter x4 -> x0, waiting for transfers between devices: 48.7 us -> none  [add_branch(): lax.psum_scatter(partial_value.astype(jnp.bfloat16), 'head', scatter_dime...]
    all_gather x4 -> x0, blocking collectives: 48.5 us -> none  [normed_full(): lax.all_gather(stream.astype(jnp.float32).astype(jnp.bfloat16), 'head', a...]
    dot_general x9 -> x0, matrix products: 46.9 us -> none  [the longest x3 23.6 us: body(): jnp.dot(context, output_weights[section], preferred_element_type=jnp.floa...]
    dot_general x8 -> x5, matrix products: 31.1 us -> 8.44 us  [project(): jnp.dot(inputs, weight, preferred_element_type=jnp.float32)]
  transfers between devices with their start and end apart: 10 -> 61, of which waited for: 7 -> 23; matrix products, arithmetic and copies ran while one was open for 13% -> 10% of each run, Pallas kernels for 0% -> 13%
where the time goes in v1:
time: 416 us; the launch traced here: 415 us
  waiting for transfers between devices  204 us (49%)
  starting transfers between devices  62 us (15%)
  Pallas kernels  58.4 us (14%)
  local copies, waits for them, and re-layouts  34.8 us (8%)
  other arithmetic  22.9 us (6%)
  matrix products  17.4 us (4%)
  between operations  15 us (4%)
    ppermute x21, waiting for transfers between devices, ring(): to_right = lax.ppermute(to_right, 'seq', rightward)  110 us
    ppermute x21, waiting for transfers between devices, ring(): to_left = lax.ppermute(to_left, 'seq', leftward)  61.4 us
    pallas_call x3, Pallas kernels, listed_attention(): pl.pallas_call(functools.partial(listed_kernel, group), grid_spec=spec, o...  32.2 us
    ppermute x5, waiting for transfers between devices, head_shift(): lax.ppermute(value, 'head', [(i, (i + k) % head_count) for i in range(hea...  31 us
    ppermute x21, starting transfers between devices, ring(): to_left = lax.ppermute(to_left, 'seq', leftward)  28.7 us
    ppermute x21, starting transfers between devices, ring(): to_right = lax.ppermute(to_right, 'seq', rightward)  17.8 us
    pallas_call x3, Pallas kernels, query_project(): pl.pallas_call(functools.partial(query_kernel, len(pieces)), grid=(column...  13.3 us
    pallas_call x3, Pallas kernels, output_project(): pl.pallas_call(functools.partial(output_kernel, len(pieces)), out_shape=j...  12.9 us
  transfers between devices with their start and end apart: 61, of which 23 were waited for; matrix products, arithmetic and copies ran while one was open for 10% of the time, Pallas kernels for 13%

profile of v1, /device:TPU:0, one launch (start us, length us, event | category | flops | bytes accessed | tf_op | source)
XLA Modules:
  0.0 415.0 jit_solution(9513282159993093220)
XLA Ops:
  6.5 3.0 collective-permute-start
  10.2 1.6 fusion.71
  14.3 4.5 %collective-permute-done = bf16[128,1536]{1,0:T(8,128)(2,1)S(1)} collective-permute-done((bf16[128,1536]{1,0:T(8,128)(2,1)}, bf16[128,1536]{1,0:T(8,128)(2,1)S(1)}, u32[]{:S(2)}, u32[]{:S(2)}) %collective-permute-start) | collective-permute-done | bytes 393248 | tf_op jit(solution)/shard_map/ppermute | solution.py:194
  21.8 2.7 fusion.19
  24.4 3.0 fusion.22
  28.9 4.3 %collective-permute-start.2 = (bf16[128,512]{1,0:T(8,128)(2,1)S(1)}, bf16[128,512]{1,0:T(8,128)(2,1)S(1)}, u32[]{:S(2)}, u32[]{:S(2)}) collective-permute-start(bf16[128,512]{1,0:T(8,128)(2,1)S(1)} %fusion.22), channel_id=1, source_target_pairs={{0,2},{2,4},{4,6},{6,8},{8,10},{10,12},{12,14},{14,16},{16,18},{18... | collective-permute-start | bytes 393224 | tf_op jit(solution)/shard_map/ppermute | solution.py:250
  33.2 1.6 convolution_convert_fusion.1
  35.5 2.0 fusion.72
  37.5 1.7 convolution_convert_fusion.2
  39.3 5.3 %convolution_convert_fusion = bf16[128,3072]{1,0:T(8,128)(2,1)S(1)} fusion(bf16[128,1536]{0,1:T(8,128)(2,1)S(1)} %bitcast.148, bf16[1536,3072]{1,0:T(8,128)(2,1)} %param.21), kind=kOutput, calls=%fused_computation.14 | convolution fusion | flops 1208352768 | bytes 10616832 | tf_op jit(solution)/shard_map/dot_general | solution.py:270
  44.6 1.6 collective-permute-start.3
  46.1 17.9 %collective-permute-done.3 = bf16[128,3072]{1,0:T(8,128)(2,1)S(1)} collective-permute-done((bf16[128,3072]{1,0:T(8,128)(2,1)S(1)}, bf16[128,3072]{1,0:T(8,128)(2,1)S(1)}, u32[]{:S(2)}, u32[]{:S(2)}) %collective-permute-start.3) | collective-permute-done | bytes 786464 | tf_op jit(solution)/shard_map/ppermute | solution.py:194
  67.1 1.6 slice_bitcast_fusion.1
  68.7 1.6 collective-permute-start.5
  73.4 2.5 slice_bitcast_fusion
  75.9 16.2 %collective-permute-done.5.refs_1_ = bf16[192,1536]{1,0:T(8,128)(2,1)} collective-permute-done((bf16[192,1536]{1,0:T(8,128)(2,1)S(1)}, bf16[192,1536]{1,0:T(8,128)(2,1)}, u32[]{:S(2)}, u32[]{:S(2)}) %collective-permute-start.5) | collective-permute-done | bytes 589856 | tf_op jit(solution)/shard_map/ppermute | solution.py:216
  92.2 3.2 collective-permute-start.15
  95.3 2.0 collective-permute-start.6
  97.3 3.0 copy.34
  100.4 2.9 gather_fusion.7
  103.3 2.1 broadcast_select_fusion.1
  105.6 32.3 %collective-permute-done.9.refs_6_ = bf16[192,1536]{1,0:T(8,128)(2,1)} collective-permute-done((bf16[192,1536]{1,0:T(8,128)(2,1)}, bf16[192,1536]{1,0:T(8,128)(2,1)}, u32[]{:S(2)}, u32[]{:S(2)}) %collective-permute-start.9) | collective-permute-done | bytes 589856 | tf_op jit(solution)/shard_map/ppermute | solution.py:213
  138.0 2.5 collective-permute-start.10
  140.8 1.7 collective-permute-start.20
  143.6 2.9 gather_fusion.6
  147.7 5.1 %collective-permute-done.16.refs_2_ = bf16[192,1536]{1,0:T(8,128)(2,1)} collective-permute-done((bf16[192,1536]{1,0:T(8,128)(2,1)}, bf16[192,1536]{1,0:T(8,128)(2,1)}, u32[]{:S(2)}, u32[]{:S(2)}) %collective-permute-start.16) | collective-permute-done | bytes 589856 | tf_op jit(solution)/shard_map/ppermute | solution.py:216
  152.8 10.9 %collective-permute-done.20.refs_6_ = bf16[192,1536]{1,0:T(8,128)(2,1)} collective-permute-done((bf16[192,1536]{1,0:T(8,128)(2,1)}, bf16[192,1536]{1,0:T(8,128)(2,1)}, u32[]{:S(2)}, u32[]{:S(2)}) %collective-permute-start.20) | collective-permute-done | bytes 589856 | tf_op jit(solution)/shard_map/ppermute | solution.py:213
  168.4 1.4 multiply_reduce_fusion.3
  171.0 12.7 %collective-permute-done.11.refs_4_ = bf16[192,1536]{1,0:T(8,128)(2,1)S(1)} collective-permute-done((bf16[192,1536]{1,0:T(8,128)(2,1)}, bf16[192,1536]{1,0:T(8,128)(2,1)S(1)}, u32[]{:S(2)}, u32[]{:S(2)}) %collective-permute-start.11) | collective-permute-done | bytes 589856 | tf_op jit(solution)/shard_map/ppermute | solution.py:213
  183.7 4.5 %query_project.3 = f32[256,1536]{1,0:T(8,128)S(1)} custom-call(bf16[1536,256]{1,0:T(8,128)(2,1)S(1)} %fusion.17.x_ref, bf16[192,1536]{1,0:T(8,128)(2,1)S(1)} %get-tuple-element.64.refs_0_, bf16[192,1536]{1,0:T(8,128)(2,1)} %collective-permute-done.5.refs_1_, bf16[192,1536]{1,0:T(8,128)(2,1)} %collective-permute-done.6.refs_2_, ...), custom_call_target="tpu_custom_call" | custom-call | flops 1207959552 | bytes 6291456 | tf_op jit(solution)/shard_map/query_project/pallas_call | solution.py:106
  188.3 2.4 collective-permute-start.21
  191.4 2.0 collective-permute-start.24
  193.6 2.2 copy-done
  195.7 10.7 %listed_attention.3.own_ref = bf16[128,1536]{1,0:T(8,128)(2,1)S(1)} custom-call(s32[16]{0:T(128)S(1)} %get-tuple-element.73.lists_ref, bf16[128,1536]{1,0:T(8,128)(2,1)S(1)} %fusion.37.q_ref, bf16[2048,1024]{1,0:T(8,128)(2,1)S(1)} %copy-done, bf16[2048,1024]{1,0:T(8,128)(2,1)S(1)} %copy-done), custom_call_target="tpu_custom_call" | custom-call | flops 1610612736 | bytes 4980736 | tf_op jit(solution)/shard_map/listed_attention/pallas_call | solution.py:77
  206.6 12.7 %collective-permute-done.24.refs_2_ = bf16[192,1536]{1,0:T(8,128)(2,1)} collective-permute-done((bf16[192,1536]{1,0:T(8,128)(2,1)}, bf16[192,1536]{1,0:T(8,128)(2,1)}, u32[]{:S(2)}, u32[]{:S(2)}) %collective-permute-start.24) | collective-permute-done | bytes 589856 | tf_op jit(solution)/shard_map/ppermute | solution.py:216
  221.6 4.5 %output_project.3 = bf16[1536,256]{1,0:T(8,128)(2,1)S(1)} custom-call(bf16[128,1536]{1,0:T(8,128)(2,1)S(1)} %listed_attention.3.own_ref, bf16[128,1536]{1,0:T(8,128)(2,1)S(1)} %collective-permute-done.14.other_ref, bf16[192,1536]{1,0:T(8,128)(2,1)} %get-tuple-element.14.refs_0_, bf16[192,1536]{1,0:T(8,128)(2,1)} %collective-permute-done.15.refs_1_, ...), custom_call_target="tpu_custom_call" | custom-call | flops 1207959552 | bytes 5505024 | tf_op jit(solution)/shard_map/output_project/pallas_call | solution.py:135
  226.0 1.6 collective-permute-start.22
  227.6 6.3 %collective-permute-done.33.refs_1_ = bf16[192,1536]{1,0:T(8,128)(2,1)} collective-permute-done((bf16[192,1536]{1,0:T(8,128)(2,1)S(1)}, bf16[192,1536]{1,0:T(8,128)(2,1)}, u32[]{:S(2)}, u32[]{:S(2)}) %collective-permute-start.33) | collective-permute-done | bytes 589856 | tf_op jit(solution)/shard_map/ppermute | solution.py:216
  238.4 10.6 %collective-permute-done.28.refs_5_ = bf16[192,1536]{1,0:T(8,128)(2,1)} collective-permute-done((bf16[192,1536]{1,0:T(8,128)(2,1)}, bf16[192,1536]{1,0:T(8,128)(2,1)}, u32[]{:S(2)}, u32[]{:S(2)}) %collective-permute-start.28) | collective-permute-done | bytes 589856 | tf_op jit(solution)/shard_map/ppermute | solution.py:213
  250.5 11.2 %collective-permute-done.38.refs_6_ = bf16[192,1536]{1,0:T(8,128)(2,1)} collective-permute-done((bf16[192,1536]{1,0:T(8,128)(2,1)}, bf16[192,1536]{1,0:T(8,128)(2,1)}, u32[]{:S(2)}, u32[]{:S(2)}) %collective-permute-start.38) | collective-permute-done | bytes 589856 | tf_op jit(solution)/shard_map/ppermute | solution.py:213
  261.7 1.7 collective-permute-start.41
  263.7 1.7 collective-permute-start.35
  265.4 2.0 multiply_reduce_fusion.1
  267.5 6.8 %collective-permute-done.29.refs_4_ = bf16[192,1536]{1,0:T(8,128)(2,1)} collective-permute-done((bf16[192,1536]{1,0:T(8,128)(2,1)}, bf16[192,1536]{1,0:T(8,128)(2,1)}, u32[]{:S(2)}, u32[]{:S(2)}) %collective-permute-start.29) | collective-permute-done | bytes 589856 | tf_op jit(solution)/shard_map/ppermute | solution.py:213
  274.3 4.8 %query_project.4 = f32[256,1536]{1,0:T(8,128)S(1)} custom-call(bf16[1536,256]{1,0:T(8,128)(2,1)S(1)} %get-tuple-element.59.x_ref, bf16[192,1536]{1,0:T(8,128)(2,1)S(1)} %get-tuple-element.15.refs_0_, bf16[192,1536]{1,0:T(8,128)(2,1)} %collective-permute-done.23.refs_1_, bf16[192,1536]{1,0:T(8,128)(2,1)} %collective-permute-done.24.refs_2_, ...), custom_call_target="tpu_custom_call" | custom-call | flops 1207959552 | bytes 6291456 | tf_op jit(solution)/shard_map/query_project/pallas_call | solution.py:106
  279.7 7.8 %collective-permute-done.35.refs_3_ = bf16[192,1536]{1,0:T(8,128)(2,1)} collective-permute-done((bf16[192,1536]{1,0:T(8,128)(2,1)}, bf16[192,1536]{1,0:T(8,128)(2,1)}, u32[]{:S(2)}, u32[]{:S(2)}) %collective-permute-start.35) | collective-permute-done | bytes 589856 | tf_op jit(solution)/shard_map/ppermute | solution.py:216
  287.9 1.7 collective-permute-start.36
  291.8 10.7 %listed_attention.4.own_ref = bf16[128,1536]{1,0:T(8,128)(2,1)S(1)} custom-call(s32[16]{0:T(128)S(1)} %get-tuple-element.75.lists_ref, bf16[128,1536]{1,0:T(8,128)(2,1)S(1)} %fusion.35.q_ref, bf16[2048,1024]{1,0:T(8,128)(2,1)S(1)} %copy-done.1, bf16[2048,1024]{1,0:T(8,128)(2,1)S(1)} %copy-done.1), custom_call_target="tpu_custom_call" | custom-call | flops 1610612736 | bytes 4980736 | tf_op jit(solution)/shard_map/listed_attention/pallas_call | solution.py:77
  303.4 10.9 %collective-permute-done.42.refs_2_ = bf16[192,1536]{1,0:T(8,128)(2,1)} collective-permute-done((bf16[192,1536]{1,0:T(8,128)(2,1)S(1)}, bf16[192,1536]{1,0:T(8,128)(2,1)}, u32[]{:S(2)}, u32[]{:S(2)}) %collective-permute-start.42) | collective-permute-done | bytes 589856 | tf_op jit(solution)/shard_map/ppermute | solution.py:216
  314.3 1.7 collective-permute-start.51
  318.8 4.3 %output_project.4 = bf16[1536,256]{1,0:T(8,128)(2,1)S(1)} custom-call(bf16[128,1536]{1,0:T(8,128)(2,1)S(1)} %copy-done.4, bf16[128,1536]{1,0:T(8,128)(2,1)S(1)} %copy-done.10, bf16[192,1536]{1,0:T(8,128)(2,1)S(1)} %get-tuple-element.16.refs_0_, bf16[192,1536]{1,0:T(8,128)(2,1)} %collective-permute-done.33.refs_1_, ...), custom_call_target="tpu_custom_call" | custom-call | flops 1207959552 | bytes 5505024 | tf_op jit(solution)/shard_map/output_project/pallas_call | solution.py:135
  323.1 1.6 collective-permute-start.40
  325.3 2.2 collective-permute-done.51.refs_1_
  327.5 2.1 collective-permute-start.52
  332.8 17.2 %collective-permute-done.46.refs_5_ = bf16[192,1536]{1,0:T(8,128)(2,1)} collective-permute-done((bf16[192,1536]{1,0:T(8,128)(2,1)}, bf16[192,1536]{1,0:T(8,128)(2,1)}, u32[]{:S(2)}, u32[]{:S(2)}) %collective-permute-start.46) | collective-permute-done | bytes 589856 | tf_op jit(solution)/shard_map/ppermute | solution.py:213
  351.3 1.9 collective-permute-start.53
  353.2 2.4 multiply_reduce_fusion
  356.8 6.0 %collective-permute-done.47.refs_4_ = bf16[192,1536]{1,0:T(8,128)(2,1)S(1)} collective-permute-done((bf16[192,1536]{1,0:T(8,128)(2,1)}, bf16[192,1536]{1,0:T(8,128)(2,1)S(1)}, u32[]{:S(2)}, u32[]{:S(2)}) %collective-permute-start.47) | collective-permute-done | bytes 589856 | tf_op jit(solution)/shard_map/ppermute | solution.py:213
  362.8 4.1 query_project.5
  372.4 2.2 copy-done.2
  374.6 10.7 %listed_attention.5.own_ref = bf16[128,1536]{1,0:T(8,128)(2,1)S(1)} custom-call(s32[16]{0:T(128)S(1)} %get-tuple-element.74.lists_ref, bf16[128,1536]{1,0:T(8,128)(2,1)S(1)} %fusion.33.q_ref, bf16[2048,1024]{1,0:T(8,128)(2,1)S(1)} %copy-done.2, bf16[2048,1024]{1,0:T(8,128)(2,1)S(1)} %copy-done.2), custom_call_target="tpu_custom_call" | custom-call | flops 1610612736 | bytes 4980736 | tf_op jit(solution)/shard_map/listed_attention/pallas_call | solution.py:77
  387.1 4.1 output_project.5
  395.5 8.5 %collective-permute-done.58 = bf16[4,192,256]{2,1,0:T(8,128)(2,1)S(1)} collective-permute-done((bf16[4,192,256]{2,1,0:T(8,128)(2,1)}, bf16[4,192,256]{2,1,0:T(8,128)(2,1)S(1)}, u32[]{:S(2)}, u32[]{:S(2)}) %collective-permute-start.58) | collective-permute-done | bytes 393248 | tf_op jit(solution)/shard_map/ppermute | solution.py:194
  404.6 1.5 collective-permute-done.59
  (241 shorter events, 59.2 us)
Async XLA Ops:
  6.5 187.0 %all-gather.2.cloned.1.call-start = ((), (), s32[]{:S(2)}) async-start(), calls=%async_computation | async-start | bytes 4456448 | tf_op jit(solution)/shard_map/all_gather | solution.py:277
  6.5 12.3 %collective-permute-start = (bf16[128,1536]{1,0:T(8,128)(2,1)}, bf16[128,1536]{1,0:T(8,128)(2,1)S(1)}, u32[]{:S(2)}, u32[]{:S(2)}) collective-permute-start(bf16[128,1536]{1,0:T(8,128)(2,1)} %param.16), channel_id=1, source_target_pairs={{0,1},{1,0},{2,3},{3,2},{4,5},{5,4},{6,7},{7,6},{8,9},{9,8},{10,11... | collective-permute-start | bytes 1179656 | tf_op jit(solution)/shard_map/ppermute | solution.py:194
  27.5 7.5 %collective-permute-start.1 = (bf16[128,512]{1,0:T(8,128)(2,1)S(1)}, bf16[128,512]{1,0:T(8,128)(2,1)S(1)}, u32[]{:S(2)}, u32[]{:S(2)}) collective-permute-start(bf16[128,512]{1,0:T(8,128)(2,1)S(1)} %fusion.19), channel_id=1, source_target_pairs={{0,2},{2,4},{4,6},{6,8},{8,10},{10,12},{12,14},{14,16},{16,18},{18... | collective-permute-start | bytes 393224 | tf_op jit(solution)/shard_map/ppermute | solution.py:251
  28.9 6.4 %collective-permute-start.2 = (bf16[128,512]{1,0:T(8,128)(2,1)S(1)}, bf16[128,512]{1,0:T(8,128)(2,1)S(1)}, u32[]{:S(2)}, u32[]{:S(2)}) collective-permute-start(bf16[128,512]{1,0:T(8,128)(2,1)S(1)} %fusion.22), channel_id=1, source_target_pairs={{0,2},{2,4},{4,6},{6,8},{8,10},{10,12},{12,14},{14,16},{16,18},{18... | collective-permute-start | bytes 393224 | tf_op jit(solution)/shard_map/ppermute | solution.py:250
  39.3 25.3 %slice-start = ((s8[6291456]{0:T(1024)(128)(4,1)}), s8[4194304]{0:T(1024)(128)(4,1)S(1)}, s32[]{:S(2)}) async-start(s8[6291456]{0:T(1024)(128)(4,1)} %bitcast.159), calls=%async_computation.1 | async-start | bytes 8388608
  39.3 25.3 %slice-start.1 = ((s8[6291456]{0:T(1024)(128)(4,1)}), s8[2097152]{0:T(1024)(128)(4,1)S(1)}, s32[]{:S(2)}) async-start(s8[6291456]{0:T(1024)(128)(4,1)} %bitcast.159), calls=%async_computation.2 | async-start | bytes 4194304
  44.5 20.0 %copy-start.19 = (f32[1,3072]{1,0:T(1,128)S(1)}, f32[1,3072]{1,0:T(1,128)}, u32[]{:S(2)}) copy-start(f32[1,3072]{1,0:T(1,128)} %get-tuple-element.70) | copy-start | bytes 36868
  44.6 19.5 %collective-permute-start.3 = (bf16[128,3072]{1,0:T(8,128)(2,1)S(1)}, bf16[128,3072]{1,0:T(8,128)(2,1)S(1)}, u32[]{:S(2)}, u32[]{:S(2)}) collective-permute-start(bf16[128,3072]{1,0:T(8,128)(2,1)S(1)} %convolution_convert_fusion), channel_id=1, source_target_pairs={{0,1},{1,0},{2,3},{3,2},{4,5},{5,4},{6,7},{7,6},{8,9},{9,8},{10,11... | collective-permute-start | bytes 2359304 | tf_op jit(solution)/shard_map/ppermute | solution.py:194
  68.7 23.4 %collective-permute-start.5 = (bf16[192,1536]{1,0:T(8,128)(2,1)S(1)}, bf16[192,1536]{1,0:T(8,128)(2,1)}, u32[]{:S(2)}, u32[]{:S(2)}) collective-permute-start(bf16[192,1536]{1,0:T(8,128)(2,1)S(1)} %get-tuple-element.64.refs_0_), channel_id=1, source_target_pairs={{0,4},{8,0},{16,8},{24,16},{28,24},{20,28},{12,20},{4,12},{2,6},{1... | collective-permute-start | bytes 1769480 | tf_op jit(solution)/shard_map/ppermute | solution.py:216
  70.3 21.8 %collective-permute-start.8 = (bf16[192,1536]{1,0:T(8,128)(2,1)S(1)}, bf16[192,1536]{1,0:T(8,128)(2,1)}, u32[]{:S(2)}, u32[]{:S(2)}) collective-permute-start(bf16[192,1536]{1,0:T(8,128)(2,1)S(1)} %get-tuple-element.64.refs_0_), channel_id=1, source_target_pairs={{0,8},{8,16},{16,24},{24,28},{28,20},{20,12},{12,4},{4,0},{2,10},{... | collective-permute-start | bytes 1769480 | tf_op jit(solution)/shard_map/ppermute | solution.py:213
  92.2 48.3 %collective-permute-start.15 = (bf16[192,1536]{1,0:T(8,128)(2,1)}, bf16[192,1536]{1,0:T(8,128)(2,1)}, u32[]{:S(2)}, u32[]{:S(2)}) collective-permute-start(bf16[192,1536]{1,0:T(8,128)(2,1)} %get-tuple-element.14.refs_0_), channel_id=1, source_target_pairs={{0,4},{8,0},{16,8},{24,16},{28,24},{20,28},{12,20},{4,12},{2,6},{1... | collective-permute-start | bytes 1769480 | tf_op jit(solution)/shard_map/ppermute | solution.py:216
  95.3 45.5 %collective-permute-start.19 = (bf16[192,1536]{1,0:T(8,128)(2,1)}, bf16[192,1536]{1,0:T(8,128)(2,1)}, u32[]{:S(2)}, u32[]{:S(2)}) collective-permute-start(bf16[192,1536]{1,0:T(8,128)(2,1)} %get-tuple-element.14.refs_0_), channel_id=1, source_target_pairs={{0,8},{8,16},{16,24},{24,28},{28,20},{20,12},{12,4},{4,0},{2,10},{... | collective-permute-start | bytes 1769480 | tf_op jit(solution)/shard_map/ppermute | solution.py:213
  95.3 47.8 %collective-permute-start.6 = (bf16[192,1536]{1,0:T(8,128)(2,1)}, bf16[192,1536]{1,0:T(8,128)(2,1)}, u32[]{:S(2)}, u32[]{:S(2)}) collective-permute-start(bf16[192,1536]{1,0:T(8,128)(2,1)} %collective-permute-done.5.refs_1_), channel_id=1, source_target_pairs={{0,4},{8,0},{16,8},{24,16},{28,24},{20,28},{12,20},{4,12},{2,6},{1... | collective-permute-start | bytes 1769480 | tf_op jit(solution)/shard_map/ppermute | solution.py:216
  97.3 40.6 %collective-permute-start.9 = (bf16[192,1536]{1,0:T(8,128)(2,1)}, bf16[192,1536]{1,0:T(8,128)(2,1)}, u32[]{:S(2)}, u32[]{:S(2)}) collective-permute-start(bf16[192,1536]{1,0:T(8,128)(2,1)} %collective-permute-done.8.refs_7_), channel_id=1, source_target_pairs={{0,8},{8,16},{16,24},{24,28},{28,20},{20,12},{12,4},{4,0},{2,10},{... | collective-permute-start | bytes 1769480 | tf_op jit(solution)/shard_map/ppermute | solution.py:213
  105.4 62.1 %collective-permute-start.4 = (f32[8,192,128]{2,1,0:T(8,128)}, f32[8,192,128]{2,1,0:T(8,128)}, u32[]{:S(2)}, u32[]{:S(2)}) collective-permute-start(f32[8,192,128]{2,1,0:T(8,128)} %broadcast_select_fusion.1), channel_id=1, source_target_pairs={{0,2},{2,0},{4,6},{6,4},{8,10},{10,8},{12,14},{14,12},{16,18},{18,... | collective-permute-start | bytes 2359304 | tf_op jit(solution)/shard_map/ppermute | solution.py:191
  138.0 28.2 %collective-permute-start.10 = (bf16[192,1536]{1,0:T(8,128)(2,1)}, bf16[192,1536]{1,0:T(8,128)(2,1)}, u32[]{:S(2)}, u32[]{:S(2)}) collective-permute-start(bf16[192,1536]{1,0:T(8,128)(2,1)} %collective-permute-done.9.refs_6_), channel_id=1, source_target_pairs={{0,8},{8,16},{16,24},{24,28},{28,20},{20,12},{12,4},{4,0},{2,10},{... | collective-permute-start | bytes 1769480 | tf_op jit(solution)/shard_map/ppermute | solution.py:213
  140.4 12.4 %collective-permute-start.16 = (bf16[192,1536]{1,0:T(8,128)(2,1)}, bf16[192,1536]{1,0:T(8,128)(2,1)}, u32[]{:S(2)}, u32[]{:S(2)}) collective-permute-start(bf16[192,1536]{1,0:T(8,128)(2,1)} %collective-permute-done.15.refs_1_), channel_id=1, source_target_pairs={{0,4},{8,0},{16,8},{24,16},{28,24},{20,28},{12,20},{4,12},{2,6},{1... | collective-permute-start | bytes 1769480 | tf_op jit(solution)/shard_map/ppermute | solution.py:216
  140.8 22.9 %collective-permute-start.20 = (bf16[192,1536]{1,0:T(8,128)(2,1)}, bf16[192,1536]{1,0:T(8,128)(2,1)}, u32[]{:S(2)}, u32[]{:S(2)}) collective-permute-start(bf16[192,1536]{1,0:T(8,128)(2,1)} %collective-permute-done.19.refs_7_), channel_id=1, source_target_pairs={{0,8},{8,16},{16,24},{24,28},{28,20},{20,12},{12,4},{4,0},{2,10},{... | collective-permute-start | bytes 1769480 | tf_op jit(solution)/shard_map/ppermute | solution.py:213
  143.1 27.0 %collective-permute-start.7 = (bf16[192,1536]{1,0:T(8,128)(2,1)}, bf16[192,1536]{1,0:T(8,128)(2,1)}, u32[]{:S(2)}, u32[]{:S(2)}) collective-permute-start(bf16[192,1536]{1,0:T(8,128)(2,1)} %collective-permute-done.6.refs_2_), channel_id=1, source_target_pairs={{0,4},{8,0},{16,8},{24,16},{28,24},{20,28},{12,20},{4,12},{2,6},{1... | collective-permute-start | bytes 1769480 | tf_op jit(solution)/shard_map/ppermute | solution.py:216
  163.7 27.7 %collective-permute-start.23 = (bf16[192,1536]{1,0:T(8,128)(2,1)S(1)}, bf16[192,1536]{1,0:T(8,128)(2,1)}, u32[]{:S(2)}, u32[]{:S(2)}) collective-permute-start(bf16[192,1536]{1,0:T(8,128)(2,1)S(1)} %get-tuple-element.15.refs_0_), channel_id=1, source_target_pairs={{0,4},{8,0},{16,8},{24,16},{28,24},{20,28},{12,20},{4,12},{2,6},{1... | collective-permute-start | bytes 1769480 | tf_op jit(solution)/shard_map/ppermute | solution.py:216
  165.0 28.4 %collective-permute-start.26 = (bf16[192,1536]{1,0:T(8,128)(2,1)S(1)}, bf16[192,1536]{1,0:T(8,128)(2,1)}, u32[]{:S(2)}, u32[]{:S(2)}) collective-permute-start(bf16[192,1536]{1,0:T(8,128)(2,1)S(1)} %get-tuple-element.15.refs_0_), channel_id=1, source_target_pairs={{0,8},{8,16},{16,24},{24,28},{28,20},{20,12},{12,4},{4,0},{2,10},{... | collective-permute-start | bytes 1769480 | tf_op jit(solution)/shard_map/ppermute | solution.py:213
  166.2 24.6 %collective-permute-start.17 = (bf16[192,1536]{1,0:T(8,128)(2,1)}, bf16[192,1536]{1,0:T(8,128)(2,1)}, u32[]{:S(2)}, u32[]{:S(2)}) collective-permute-start(bf16[192,1536]{1,0:T(8,128)(2,1)} %collective-permute-done.16.refs_2_), channel_id=1, source_target_pairs={{0,4},{8,0},{16,8},{24,16},{28,24},{20,28},{12,20},{4,12},{2,6},{1... | collective-permute-start | bytes 1769480 | tf_op jit(solution)/shard_map/ppermute | solution.py:216
  167.5 16.2 %collective-permute-start.11 = (bf16[192,1536]{1,0:T(8,128)(2,1)}, bf16[192,1536]{1,0:T(8,128)(2,1)S(1)}, u32[]{:S(2)}, u32[]{:S(2)}) collective-permute-start(bf16[192,1536]{1,0:T(8,128)(2,1)} %collective-permute-done.10.refs_5_), channel_id=1, source_target_pairs={{0,8},{8,16},{16,24},{24,28},{28,20},{20,12},{12,4},{4,0},{2,10},{... | collective-permute-start | bytes 1769480 | tf_op jit(solution)/shard_map/ppermute | solution.py:213
  170.1 18.2 %collective-permute-start.13 = (f32[128]{0:T(128)S(1)}, f32[128]{0:T(128)S(1)}, u32[]{:S(2)}, u32[]{:S(2)}) collective-permute-start(f32[128]{0:T(128)S(1)} %slice.111), channel_id=1, source_target_pairs={{0,2},{2,0},{4,6},{6,4},{8,10},{10,8},{12,14},{14,12},{16,18},{18,... | collective-permute-start | bytes 1544 | tf_op jit(solution)/shard_map/ppermute | solution.py:191
  188.2 5.2 %collective-permute-start.12 = (bf16[128,1536]{1,0:T(8,128)(2,1)S(1)}, bf16[128,1536]{1,0:T(8,128)(2,1)S(1)}, u32[]{:S(2)}, u32[]{:S(2)}) collective-permute-start(bf16[128,1536]{1,0:T(8,128)(2,1)S(1)} %slice.230), channel_id=1, source_target_pairs={{0,2},{2,0},{4,6},{6,4},{8,10},{10,8},{12,14},{14,12},{16,18},{18,... | collective-permute-start | bytes 1179656 | tf_op jit(solution)/shard_map/ppermute | solution.py:191
  188.3 32.9 %collective-permute-start.21 = (bf16[192,1536]{1,0:T(8,128)(2,1)}, bf16[192,1536]{1,0:T(8,128)(2,1)}, u32[]{:S(2)}, u32[]{:S(2)}) collective-permute-start(bf16[192,1536]{1,0:T(8,128)(2,1)} %collective-permute-done.20.refs_6_), channel_id=1, source_target_pairs={{0,8},{8,16},{16,24},{24,28},{28,20},{20,12},{12,4},{4,0},{2,10},{... | collective-permute-start | bytes 1769480 | tf_op jit(solution)/shard_map/ppermute | solution.py:213
  190.8 30.8 %collective-permute-start.18 = (bf16[192,1536]{1,0:T(8,128)(2,1)}, bf16[192,1536]{1,0:T(8,128)(2,1)}, u32[]{:S(2)}, u32[]{:S(2)}) collective-permute-start(bf16[192,1536]{1,0:T(8,128)(2,1)} %collective-permute-done.17.refs_3_), channel_id=1, source_target_pairs={{0,4},{8,0},{16,8},{24,16},{28,24},{20,28},{12,20},{4,12},{2,6},{1... | collective-permute-start | bytes 1769480 | tf_op jit(solution)/shard_map/ppermute | solution.py:216
  191.4 27.9 %collective-permute-start.24 = (bf16[192,1536]{1,0:T(8,128)(2,1)}, bf16[192,1536]{1,0:T(8,128)(2,1)}, u32[]{:S(2)}, u32[]{:S(2)}) collective-permute-start(bf16[192,1536]{1,0:T(8,128)(2,1)} %collective-permute-done.23.refs_1_), channel_id=1, source_target_pairs={{0,4},{8,0},{16,8},{24,16},{28,24},{20,28},{12,20},{4,12},{2,6},{1... | collective-permute-start | bytes 1769480 | tf_op jit(solution)/shard_map/ppermute | solution.py:216
  193.4 25.9 %collective-permute-start.27 = (bf16[192,1536]{1,0:T(8,128)(2,1)}, bf16[192,1536]{1,0:T(8,128)(2,1)}, u32[]{:S(2)}, u32[]{:S(2)}) collective-permute-start(bf16[192,1536]{1,0:T(8,128)(2,1)} %collective-permute-done.26.refs_7_), channel_id=1, source_target_pairs={{0,8},{8,16},{16,24},{24,28},{28,20},{20,12},{12,4},{4,0},{2,10},{... | collective-permute-start | bytes 1769480 | tf_op jit(solution)/shard_map/ppermute | solution.py:213
  206.5 15.1 %collective-permute-start.14 = (bf16[128,1536]{1,0:T(8,128)(2,1)S(1)}, bf16[128,1536]{1,0:T(8,128)(2,1)S(1)}, u32[]{:S(2)}, u32[]{:S(2)}) collective-permute-start(bf16[128,1536]{1,0:T(8,128)(2,1)S(1)} %listed_attention.3.own_ref), channel_id=1, source_target_pairs={{0,2},{2,0},{4,6},{6,4},{8,10},{10,8},{12,14},{14,12},{16,18},{18,... | collective-permute-start | bytes 1179656 | tf_op jit(solution)/shard_map/ppermute | solution.py:191
  219.2 14.7 %collective-permute-start.33 = (bf16[192,1536]{1,0:T(8,128)(2,1)S(1)}, bf16[192,1536]{1,0:T(8,128)(2,1)}, u32[]{:S(2)}, u32[]{:S(2)}) collective-permute-start(bf16[192,1536]{1,0:T(8,128)(2,1)S(1)} %get-tuple-element.16.refs_0_), channel_id=1, source_target_pairs={{0,4},{8,0},{16,8},{24,16},{28,24},{20,28},{12,20},{4,12},{2,6},{1... | collective-permute-start | bytes 1769480 | tf_op jit(solution)/shard_map/ppermute | solution.py:216
  220.0 16.4 %collective-permute-start.37 = (bf16[192,1536]{1,0:T(8,128)(2,1)S(1)}, bf16[192,1536]{1,0:T(8,128)(2,1)}, u32[]{:S(2)}, u32[]{:S(2)}) collective-permute-start(bf16[192,1536]{1,0:T(8,128)(2,1)S(1)} %get-tuple-element.16.refs_0_), channel_id=1, source_target_pairs={{0,8},{8,16},{16,24},{24,28},{28,20},{20,12},{12,4},{4,0},{2,10},{... | collective-permute-start | bytes 1769480 | tf_op jit(solution)/shard_map/ppermute | solution.py:213
  221.3 27.8 %collective-permute-start.28 = (bf16[192,1536]{1,0:T(8,128)(2,1)}, bf16[192,1536]{1,0:T(8,128)(2,1)}, u32[]{:S(2)}, u32[]{:S(2)}) collective-permute-start(bf16[192,1536]{1,0:T(8,128)(2,1)} %collective-permute-done.27.refs_6_), channel_id=1, source_target_pairs={{0,8},{8,16},{16,24},{24,28},{28,20},{20,12},{12,4},{4,0},{2,10},{... | collective-permute-start | bytes 1769480 | tf_op jit(solution)/shard_map/ppermute | solution.py:213
  226.0 37.7 %collective-permute-start.22 = (bf16[1536,256]{1,0:T(8,128)(2,1)S(1)}, bf16[1536,256]{1,0:T(8,128)(2,1)}, u32[]{:S(2)}, u32[]{:S(2)}) collective-permute-start(bf16[1536,256]{1,0:T(8,128)(2,1)S(1)} %output_project.3), channel_id=1, source_target_pairs={{0,1},{1,0},{2,3},{3,2},{4,5},{5,4},{6,7},{7,6},{8,9},{9,8},{10,11... | collective-permute-start | bytes 2359304 | tf_op jit(solution)/shard_map/ppermute | solution.py:194
  233.9 16.6 %collective-permute-start.34 = (bf16[192,1536]{1,0:T(8,128)(2,1)}, bf16[192,1536]{1,0:T(8,128)(2,1)}, u32[]{:S(2)}, u32[]{:S(2)}) collective-permute-start(bf16[192,1536]{1,0:T(8,128)(2,1)} %collective-permute-done.33.refs_1_), channel_id=1, source_target_pairs={{0,4},{8,0},{16,8},{24,16},{28,24},{20,28},{12,20},{4,12},{2,6},{1... | collective-permute-start | bytes 1769480 | tf_op jit(solution)/shard_map/ppermute | solution.py:216
  236.4 25.3 %collective-permute-start.38 = (bf16[192,1536]{1,0:T(8,128)(2,1)}, bf16[192,1536]{1,0:T(8,128)(2,1)}, u32[]{:S(2)}, u32[]{:S(2)}) collective-permute-start(bf16[192,1536]{1,0:T(8,128)(2,1)} %collective-permute-done.37.refs_7_), channel_id=1, source_target_pairs={{0,8},{8,16},{16,24},{24,28},{28,20},{20,12},{12,4},{4,0},{2,10},{... | collective-permute-start | bytes 1769480 | tf_op jit(solution)/shard_map/ppermute | solution.py:213
  237.6 29.9 %collective-permute-start.25 = (bf16[192,1536]{1,0:T(8,128)(2,1)}, bf16[192,1536]{1,0:T(8,128)(2,1)}, u32[]{:S(2)}, u32[]{:S(2)}) collective-permute-start(bf16[192,1536]{1,0:T(8,128)(2,1)} %collective-permute-done.24.refs_2_), channel_id=1, source_target_pairs={{0,4},{8,0},{16,8},{24,16},{28,24},{20,28},{12,20},{4,12},{2,6},{1... | collective-permute-start | bytes 1769480 | tf_op jit(solution)/shard_map/ppermute | solution.py:216
  249.0 25.3 %collective-permute-start.29 = (bf16[192,1536]{1,0:T(8,128)(2,1)}, bf16[192,1536]{1,0:T(8,128)(2,1)}, u32[]{:S(2)}, u32[]{:S(2)}) collective-permute-start(bf16[192,1536]{1,0:T(8,128)(2,1)} %collective-permute-done.28.refs_5_), channel_id=1, source_target_pairs={{0,8},{8,16},{16,24},{24,28},{28,20},{20,12},{12,4},{4,0},{2,10},{... | collective-permute-start | bytes 1769480 | tf_op jit(solution)/shard_map/ppermute | solution.py:213
  261.7 26.2 %collective-permute-start.41 = (bf16[192,1536]{1,0:T(8,128)(2,1)S(1)}, bf16[192,1536]{1,0:T(8,128)(2,1)S(1)}, u32[]{:S(2)}, u32[]{:S(2)}) collective-permute-start(bf16[192,1536]{1,0:T(8,128)(2,1)S(1)} %get-tuple-element.17.refs_0_), channel_id=1, source_target_pairs={{0,4},{8,0},{16,8},{24,16},{28,24},{20,28},{12,20},{4,12},{2,6},{1... | collective-permute-start | bytes 1769480 | tf_op jit(solution)/shard_map/ppermute | solution.py:216
  263.4 26.2 %collective-permute-start.44 = (bf16[192,1536]{1,0:T(8,128)(2,1)S(1)}, bf16[192,1536]{1,0:T(8,128)(2,1)S(1)}, u32[]{:S(2)}, u32[]{:S(2)}) collective-permute-start(bf16[192,1536]{1,0:T(8,128)(2,1)S(1)} %get-tuple-element.17.refs_0_), channel_id=1, source_target_pairs={{0,8},{8,16},{16,24},{24,28},{28,20},{20,12},{12,4},{4,0},{2,10},{... | collective-permute-start | bytes 1769480 | tf_op jit(solution)/shard_map/ppermute | solution.py:213
  263.7 23.8 %collective-permute-start.35 = (bf16[192,1536]{1,0:T(8,128)(2,1)}, bf16[192,1536]{1,0:T(8,128)(2,1)}, u32[]{:S(2)}, u32[]{:S(2)}) collective-permute-start(bf16[192,1536]{1,0:T(8,128)(2,1)} %collective-permute-done.34.refs_2_), channel_id=1, source_target_pairs={{0,4},{8,0},{16,8},{24,16},{28,24},{20,28},{12,20},{4,12},{2,6},{1... | collective-permute-start | bytes 1769480 | tf_op jit(solution)/shard_map/ppermute | solution.py:216
  279.1 12.5 %collective-permute-start.30 = (bf16[128,1536]{1,0:T(8,128)(2,1)S(1)}, bf16[128,1536]{1,0:T(8,128)(2,1)S(1)}, u32[]{:S(2)}, u32[]{:S(2)}) collective-permute-start(bf16[128,1536]{1,0:T(8,128)(2,1)S(1)} %slice.229), channel_id=1, source_target_pairs={{0,2},{2,0},{4,6},{6,4},{8,10},{10,8},{12,14},{14,12},{16,18},{18,... | collective-permute-start | bytes 1179656 | tf_op jit(solution)/shard_map/ppermute | solution.py:191
  279.2 11.2 %collective-permute-start.31 = (f32[128]{0:T(128)S(1)}, f32[128]{0:T(128)S(1)}, u32[]{:S(2)}, u32[]{:S(2)}) collective-permute-start(f32[128]{0:T(128)S(1)} %slice.122), channel_id=1, source_target_pairs={{0,2},{2,0},{4,6},{6,4},{8,10},{10,8},{12,14},{14,12},{16,18},{18,... | collective-permute-start | bytes 1544 | tf_op jit(solution)/shard_map/ppermute | solution.py:191
  287.5 28.5 %collective-permute-start.39 = (bf16[192,1536]{1,0:T(8,128)(2,1)}, bf16[192,1536]{1,0:T(8,128)(2,1)}, u32[]{:S(2)}, u32[]{:S(2)}) collective-permute-start(bf16[192,1536]{1,0:T(8,128)(2,1)} %collective-permute-done.38.refs_6_), channel_id=1, source_target_pairs={{0,8},{8,16},{16,24},{24,28},{28,20},{20,12},{12,4},{4,0},{2,10},{... | collective-permute-start | bytes 1769480 | tf_op jit(solution)/shard_map/ppermute | solution.py:213
  287.9 28.1 %collective-permute-start.36 = (bf16[192,1536]{1,0:T(8,128)(2,1)}, bf16[192,1536]{1,0:T(8,128)(2,1)}, u32[]{:S(2)}, u32[]{:S(2)}) collective-permute-start(bf16[192,1536]{1,0:T(8,128)(2,1)} %collective-permute-done.35.refs_3_), channel_id=1, source_target_pairs={{0,4},{8,0},{16,8},{24,16},{28,24},{20,28},{12,20},{4,12},{2,6},{1... | collective-permute-start | bytes 1769480 | tf_op jit(solution)/shard_map/ppermute | solution.py:216
  289.6 24.7 %collective-permute-start.42 = (bf16[192,1536]{1,0:T(8,128)(2,1)S(1)}, bf16[192,1536]{1,0:T(8,128)(2,1)}, u32[]{:S(2)}, u32[]{:S(2)}) collective-permute-start(bf16[192,1536]{1,0:T(8,128)(2,1)S(1)} %collective-permute-done.41.refs_1_), channel_id=1, source_target_pairs={{0,4},{8,0},{16,8},{24,16},{28,24},{20,28},{12,20},{4,12},{2,6},{1... | collective-permute-start | bytes 1769480 | tf_op jit(solution)/shard_map/ppermute | solution.py:216
  290.5 23.8 %collective-permute-start.45 = (bf16[192,1536]{1,0:T(8,128)(2,1)S(1)}, bf16[192,1536]{1,0:T(8,128)(2,1)}, u32[]{:S(2)}, u32[]{:S(2)}) collective-permute-start(bf16[192,1536]{1,0:T(8,128)(2,1)S(1)} %collective-permute-done.44.refs_7_), channel_id=1, source_target_pairs={{0,8},{8,16},{16,24},{24,28},{28,20},{20,12},{12,4},{4,0},{2,10},{... | collective-permute-start | bytes 1769480 | tf_op jit(solution)/shard_map/ppermute | solution.py:213
  302.5 13.5 %collective-permute-start.32 = (bf16[128,1536]{1,0:T(8,128)(2,1)S(1)}, bf16[128,1536]{1,0:T(8,128)(2,1)S(1)}, u32[]{:S(2)}, u32[]{:S(2)}) collective-permute-start(bf16[128,1536]{1,0:T(8,128)(2,1)S(1)} %listed_attention.4.own_ref), channel_id=1, source_target_pairs={{0,2},{2,0},{4,6},{6,4},{8,10},{10,8},{12,14},{14,12},{16,18},{18,... | collective-permute-start | bytes 1179656 | tf_op jit(solution)/shard_map/ppermute | solution.py:191
  314.3 13.3 %collective-permute-start.51 = (bf16[192,1536]{1,0:T(8,128)(2,1)S(1)}, bf16[192,1536]{1,0:T(8,128)(2,1)}, u32[]{:S(2)}, u32[]{:S(2)}) collective-permute-start(bf16[192,1536]{1,0:T(8,128)(2,1)S(1)} %get-tuple-element.18.refs_0_), channel_id=1, source_target_pairs={{0,4},{8,0},{16,8},{24,16},{28,24},{20,28},{12,20},{4,12},{2,6},{1... | collective-permute-start | bytes 1769480 | tf_op jit(solution)/shard_map/ppermute | solution.py:216
  323.1 30.1 %collective-permute-start.40 = (bf16[1536,256]{1,0:T(8,128)(2,1)S(1)}, bf16[1536,256]{1,0:T(8,128)(2,1)}, u32[]{:S(2)}, u32[]{:S(2)}) collective-permute-start(bf16[1536,256]{1,0:T(8,128)(2,1)S(1)} %output_project.4), channel_id=1, source_target_pairs={{0,1},{1,0},{2,3},{3,2},{4,5},{5,4},{6,7},{7,6},{8,9},{9,8},{10,11... | collective-permute-start | bytes 2359304 | tf_op jit(solution)/shard_map/ppermute | solution.py:194
  324.9 26.3 %collective-permute-start.55 = (bf16[192,1536]{1,0:T(8,128)(2,1)S(1)}, bf16[192,1536]{1,0:T(8,128)(2,1)S(1)}, u32[]{:S(2)}, u32[]{:S(2)}) collective-permute-start(bf16[192,1536]{1,0:T(8,128)(2,1)S(1)} %get-tuple-element.18.refs_0_), channel_id=1, source_target_pairs={{0,8},{8,16},{16,24},{24,28},{28,20},{20,12},{12,4},{4,0},{2,10},{... | collective-permute-start | bytes 1769480 | tf_op jit(solution)/shard_map/ppermute | solution.py:213
  325.2 24.7 %collective-permute-start.46 = (bf16[192,1536]{1,0:T(8,128)(2,1)}, bf16[192,1536]{1,0:T(8,128)(2,1)}, u32[]{:S(2)}, u32[]{:S(2)}) collective-permute-start(bf16[192,1536]{1,0:T(8,128)(2,1)} %collective-permute-done.45.refs_6_), channel_id=1, source_target_pairs={{0,8},{8,16},{16,24},{24,28},{28,20},{20,12},{12,4},{4,0},{2,10},{... | collective-permute-start | bytes 1769480 | tf_op jit(solution)/shard_map/ppermute | solution.py:213
  327.5 23.7 %collective-permute-start.52 = (bf16[192,1536]{1,0:T(8,128)(2,1)}, bf16[192,1536]{1,0:T(8,128)(2,1)}, u32[]{:S(2)}, u32[]{:S(2)}) collective-permute-start(bf16[192,1536]{1,0:T(8,128)(2,1)} %collective-permute-done.51.refs_1_), channel_id=1, source_target_pairs={{0,4},{8,0},{16,8},{24,16},{28,24},{20,28},{12,20},{4,12},{2,6},{1... | collective-permute-start | bytes 1769480 | tf_op jit(solution)/shard_map/ppermute | solution.py:216
  332.2 23.7 %collective-permute-start.43 = (bf16[192,1536]{1,0:T(8,128)(2,1)}, bf16[192,1536]{1,0:T(8,128)(2,1)S(1)}, u32[]{:S(2)}, u32[]{:S(2)}) collective-permute-start(bf16[192,1536]{1,0:T(8,128)(2,1)} %collective-permute-done.42.refs_2_), channel_id=1, source_target_pairs={{0,4},{8,0},{16,8},{24,16},{28,24},{20,28},{12,20},{4,12},{2,6},{1... | collective-permute-start | bytes 1769480 | tf_op jit(solution)/shard_map/ppermute | solution.py:216
  349.9 12.8 %collective-permute-start.47 = (bf16[192,1536]{1,0:T(8,128)(2,1)}, bf16[192,1536]{1,0:T(8,128)(2,1)S(1)}, u32[]{:S(2)}, u32[]{:S(2)}) collective-permute-start(bf16[192,1536]{1,0:T(8,128)(2,1)} %collective-permute-done.46.refs_5_), channel_id=1, source_target_pairs={{0,8},{8,16},{16,24},{24,28},{28,20},{20,12},{12,4},{4,0},{2,10},{... | collective-permute-start | bytes 1769480 | tf_op jit(solution)/shard_map/ppermute | solution.py:213
  351.2 18.0 %collective-permute-start.56 = (bf16[192,1536]{1,0:T(8,128)(2,1)S(1)}, bf16[192,1536]{1,0:T(8,128)(2,1)}, u32[]{:S(2)}, u32[]{:S(2)}) collective-permute-start(bf16[192,1536]{1,0:T(8,128)(2,1)S(1)} %collective-permute-done.55.refs_7_), channel_id=1, source_target_pairs={{0,8},{8,16},{16,24},{24,28},{28,20},{20,12},{12,4},{4,0},{2,10},{... | collective-permute-start | bytes 1769480 | tf_op jit(solution)/shard_map/ppermute | solution.py:213
  351.3 19.0 %collective-permute-start.53 = (bf16[192,1536]{1,0:T(8,128)(2,1)}, bf16[192,1536]{1,0:T(8,128)(2,1)}, u32[]{:S(2)}, u32[]{:S(2)}) collective-permute-start(bf16[192,1536]{1,0:T(8,128)(2,1)} %collective-permute-done.52.refs_2_), channel_id=1, source_target_pairs={{0,4},{8,0},{16,8},{24,16},{28,24},{20,28},{12,20},{4,12},{2,6},{1... | collective-permute-start | bytes 1769480 | tf_op jit(solution)/shard_map/ppermute | solution.py:216
  366.9 4.3 %collective-permute-start.48 = (bf16[128,1536]{1,0:T(8,128)(2,1)S(1)}, bf16[128,1536]{1,0:T(8,128)(2,1)}, u32[]{:S(2)}, u32[]{:S(2)}) collective-permute-start(bf16[128,1536]{1,0:T(8,128)(2,1)S(1)} %slice.228), channel_id=1, source_target_pairs={{0,2},{2,0},{4,6},{6,4},{8,10},{10,8},{12,14},{14,12},{16,18},{18,... | collective-permute-start | bytes 1179656 | tf_op jit(solution)/shard_map/ppermute | solution.py:191
  367.0 4.2 %collective-permute-start.49 = (f32[128]{0:T(128)S(1)}, f32[128]{0:T(128)S(1)}, u32[]{:S(2)}, u32[]{:S(2)}) collective-permute-start(f32[128]{0:T(128)S(1)} %slice.130), channel_id=1, source_target_pairs={{0,2},{2,0},{4,6},{6,4},{8,10},{10,8},{12,14},{14,12},{16,18},{18,... | collective-permute-start | bytes 1544 | tf_op jit(solution)/shard_map/ppermute | solution.py:191
  369.2 17.5 %collective-permute-start.57 = (bf16[192,1536]{1,0:T(8,128)(2,1)}, bf16[192,1536]{1,0:T(8,128)(2,1)}, u32[]{:S(2)}, u32[]{:S(2)}) collective-permute-start(bf16[192,1536]{1,0:T(8,128)(2,1)} %collective-permute-done.56.refs_6_), channel_id=1, source_target_pairs={{0,8},{8,16},{16,24},{24,28},{28,20},{20,12},{12,4},{4,0},{2,10},{... | collective-permute-start | bytes 1769480 | tf_op jit(solution)/shard_map/ppermute | solution.py:213
  370.2 16.5 %collective-permute-start.54 = (bf16[192,1536]{1,0:T(8,128)(2,1)}, bf16[192,1536]{1,0:T(8,128)(2,1)}, u32[]{:S(2)}, u32[]{:S(2)}) collective-permute-start(bf16[192,1536]{1,0:T(8,128)(2,1)} %collective-permute-done.53.refs_3_), channel_id=1, source_target_pairs={{0,4},{8,0},{16,8},{24,16},{28,24},{20,28},{12,20},{4,12},{2,6},{1... | collective-permute-start | bytes 1769480 | tf_op jit(solution)/shard_map/ppermute | solution.py:216
  385.3 1.8 collective-permute-start.50
  392.7 11.4 %collective-permute-start.58 = (bf16[4,192,256]{2,1,0:T(8,128)(2,1)}, bf16[4,192,256]{2,1,0:T(8,128)(2,1)S(1)}, u32[]{:S(2)}, u32[]{:S(2)}) collective-permute-start(bf16[4,192,256]{2,1,0:T(8,128)(2,1)} %broadcast_select_fusion.3), channel_id=1, source_target_pairs={{0,1},{1,0},{2,3},{3,2},{4,5},{5,4},{6,7},{7,6},{8,9},{9,8},{10,11... | collective-permute-start | bytes 1179656 | tf_op jit(solution)/shard_map/ppermute | solution.py:194
  404.3 1.8 collective-permute-start.59
  (24 other events, 127.1 us)
Sparse Core Ops, SparseCore 0:
  67.2 64.3 all-gather.1

commit v2 on v0

v2 whole, which is shorter than its diff:
```python
import functools

import jax
import jax.numpy as jnp
import numpy as np
from jax import lax
from jax.experimental import pallas as pl
from jax.experimental.pallas import tpu as pltpu
from jax.sharding import PartitionSpec as P

HEAD_WIDTH = 128
EPSILON = 1e-06
MASKED = -1e30
CORES = 2
SCALE = HEAD_WIDTH ** (-0.5) * 1.4426950408889634
PARAMS = pltpu.CompilerParams(vmem_limit_bytes=44 << 20)
COST = pl.CostEstimate(flops=1, bytes_accessed=1, transcendentals=0)


def dot(a, b, contract):
    return lax.dot_general(a, b, ((contract[0], contract[1]), ((), ())), preferred_element_type=jnp.float32)


def tiles(columns, at_most):
    return next(t for t in range(min(columns, at_most) // 128 * 128, 0, -128) if columns % t == 0)


def normed(values, gain_row):
    factor = lax.rsqrt(jnp.mean(values * values, axis=1, keepdims=True) + EPSILON)
    return (values * factor * gain_row).astype(jnp.bfloat16)


def whole(array):
    rank = len(array.shape)
    return pl.BlockSpec(array.shape, lambda *_: (0,) * rank)


def first_kernel(count, *refs):
    parts, gain_ref, w_ref, x_ref, o_ref = refs[:count], *refs[count:]

    @pl.when((pl.program_id(0) == 0) & (pl.program_id(1) == 0))
    def _():
        values = jnp.concatenate([p[...] for p in parts], axis=1).astype(jnp.float32)
        x_ref[...] = normed(values, gain_ref[...])

    o_ref[...] = dot(x_ref[...], w_ref[0], ((1,), (0,))).astype(o_ref.dtype)


def norm_and_pair(parts, gain, weight):
    rows = parts[0].shape[0]
    _, width, columns = weight.shape
    tile = tiles(columns, 256)
    count = columns // tile
    return pl.pallas_call(
        functools.partial(first_kernel, len(parts)),
        grid=(2, count),
        in_specs=[whole(p) for p in parts]
        + [whole(gain), pl.BlockSpec((1, width, tile), lambda i, n: (i, 0, n))],
        out_specs=[
            pl.BlockSpec((rows, width), lambda i, n: (0, 0)),
            pl.BlockSpec((rows, tile), lambda i, n: (0, i * count + n)),
        ],
        out_shape=[
            jax.ShapeDtypeStruct((rows, width), jnp.bfloat16),
            jax.ShapeDtypeStruct((rows, 2 * columns), jnp.bfloat16),
        ],
        compiler_params=PARAMS,
        cost_estimate=COST,
        name="norm_and_pair",
    )(*parts, gain, weight)


def product_kernel(x_ref, w_ref, o_ref):
    o_ref[...] = dot(x_ref[...], w_ref[...], ((1,), (0,))).astype(o_ref.dtype)


def product(inputs, weight):
    rows, width = inputs.shape
    columns = weight.shape[1]
    tile = tiles(columns, 512 if width > 2048 else 768)
    return pl.pallas_call(
        product_kernel,
        grid=(columns // tile,),
        in_specs=[whole(inputs), pl.BlockSpec((width, tile), lambda n: (0, n))],
        out_specs=pl.BlockSpec((rows, tile), lambda n: (0, n)),
        out_shape=jax.ShapeDtypeStruct((rows, columns), jnp.bfloat16),
        compiler_params=PARAMS,
        cost_estimate=COST,
        name="product",
    )(inputs, weight)


def window_kernel(group, info_ref, q_ref, kp_ref, ko_ref, vp_ref, vo_ref, o_ref):
    rows, width = ko_ref.shape
    head = pl.program_id(0)
    q = jnp.concatenate([q_ref[:, g * width : (g + 1) * width] for g in range(group)], axis=0)
    keys = jnp.concatenate([kp_ref[...], ko_ref[...]], axis=0)
    values = jnp.concatenate([vp_ref[...], vo_ref[...]], axis=0)
    s = dot(q, keys, ((1,), (1,)))
    row = lax.broadcasted_iota(jnp.int32, (rows, 2 * rows), 0)
    col = lax.broadcasted_iota(jnp.int32, (rows, 2 * rows), 1)
    offset = row + rows - col
    seen = (offset >= 0) & ((col >= rows) | (info_ref[0] > 0))
    masks = [seen & (offset < info_ref[1 + head * group + g]) for g in range(group)]
    s = jnp.concatenate(
        [jnp.where(masks[g], s[g * rows : (g + 1) * rows], MASKED) for g in range(group)], axis=0
    )
    weights = jnp.exp2((s - jnp.max(s, axis=1, keepdims=True)) * SCALE)
    total = jnp.sum(weights, axis=1, keepdims=True)
    acc = dot(weights.astype(jnp.bfloat16), values, ((1,), (0,))) / total
    for g in range(group):
        o_ref[:, g * width : (g + 1) * width] = acc[g * rows : (g + 1) * rows].astype(o_ref.dtype)


def window_attention(info, query, before, own, kv_heads):
    rows, columns = query.shape
    group = columns // (kv_heads * HEAD_WIDTH)
    queries = pl.BlockSpec((rows, group * HEAD_WIDTH), lambda h, _: (0, h))
    keys = pl.BlockSpec((rows, HEAD_WIDTH), lambda h, _: (0, h))
    values = pl.BlockSpec((rows, HEAD_WIDTH), lambda h, _: (0, kv_heads + h))
    return pl.pallas_call(
        functools.partial(window_kernel, group),
        grid_spec=pltpu.PrefetchScalarGridSpec(
            num_scalar_prefetch=1,
            grid=(kv_heads,),
            in_specs=[queries, keys, keys, values, values],
            out_specs=queries,
        ),
        out_shape=jax.ShapeDtypeStruct((rows, columns), jnp.bfloat16),
        compiler_params=PARAMS,
        cost_estimate=COST,
        name="window_attention",
    )(info, query, before, own, before, own)


def cache_kernel(count, chips, addends, ids_ref, *refs):
    parts, sums = refs[:count], refs[count : count + addends]
    gain_ref, w_ref, o_ref, mine_ref, others_ref, x_ref, t_ref = refs[count + addends :]
    shard = mine_ref.shape[0] // chips

    @pl.when((pl.program_id(0) == 0) & (pl.program_id(1) == 0))
    def _():
        values = jnp.concatenate([p[...] for p in parts], axis=1).astype(jnp.float32)
        values = values + added([ref[...] for ref in sums])
        x_ref[...] = normed(values, gain_ref[...])
        t_ref[...] = values.T

    o_ref[...] = dot(x_ref[...], w_ref[0], ((1,), (0,))).astype(o_ref.dtype)

    @pl.when((pl.program_id(0) == 1) & (pl.program_id(1) == pl.num_programs(1) - 1))
    def _():
        for j in range(chips):
            for k, ref in enumerate((mine_ref, others_ref)):
                at = pl.multiple_of(ids_ref[k * chips + j] * shard, shard)
                ref[j * shard : (j + 1) * shard, :] = t_ref[pl.ds(at, shard), :]


def cache_and_state(ids, parts, sums, gain, weight, chips):
    rows = parts[0].shape[0]
    _, width, columns = weight.shape
    tile = tiles(columns, 256)
    count = columns // tile
    held = width // CORES
    return pl.pallas_call(
        functools.partial(cache_kernel, len(parts), chips, len(sums)),
        grid_spec=pltpu.PrefetchScalarGridSpec(
            num_scalar_prefetch=1,
            grid=(2, count),
            in_specs=[whole(p) for p in parts]
            + [whole(p) for p in sums]
            + [whole(gain), pl.BlockSpec((1, width, tile), lambda i, n, _: (i, 0, n))],
            out_specs=[
                pl.BlockSpec((rows, tile), lambda i, n, _: (0, i * count + n)),
                pl.BlockSpec((held, rows), lambda i, n, _: (0, 0)),
                pl.BlockSpec((held, rows), lambda i, n, _: (0, 0)),
            ],
            scratch_shapes=[pltpu.VMEM((rows, width), jnp.bfloat16), pltpu.VMEM((width, rows), jnp.float32)],
        ),
        out_shape=[
            jax.ShapeDtypeStruct((rows, 2 * columns), jnp.bfloat16),
            jax.ShapeDtypeStruct((held, rows), jnp.float32),
            jax.ShapeDtypeStruct((held, rows), jnp.float32),
        ],
        compiler_params=PARAMS,
        cost_estimate=COST,
        name="cache_and_state",
    )(ids, *parts, *sums, gain, weight)


def fetch(ids_ref, refs, held, arrived):
    count = arrived.shape[0]
    shard = held.shape[0] // count
    copies = []
    for j in range(count):
        source = refs[j].at[0] if len(refs) > 1 else refs[0].at[ids_ref[j]]
        copies.append(pltpu.make_async_copy(source, held.at[pl.ds(j * shard, shard)], arrived.at[j]))
        copies[-1].start()
    return copies


def added(sums):
    total = sums[0].astype(jnp.float32)
    for value in sums[1:]:
        total = total + value.astype(jnp.float32)
    return total


def query_kernel(states, addends, ids_ref, *refs):
    state_refs, sums = refs[:states], refs[states : states + addends]
    gain_ref, *refs = refs[states + addends :]
    *w_refs, new_ref, own_ref, twin_ref, square_ref, x_ref, held, arrived = refs
    tokens, features = x_ref.shape
    rows = tokens // CORES
    columns = own_ref.shape[1]
    tile = tiles(columns, 512)
    copies = fetch(ids_ref, w_refs, held, arrived)
    squares = jnp.zeros((tokens, 1), jnp.float32)
    part = tiles(features, 512)
    for at in range(0, features, part):
        span = slice(at, at + part)
        value = jnp.concatenate([ref[span, :] for ref in state_refs], axis=1)
        if sums:
            value = value + added([ref[span, :] for ref in sums])
        new_ref[span, :] = value
        turned = value.T
        squares = squares + jnp.sum(turned * turned, axis=1, keepdims=True)
        x_ref[:, span] = (turned * gain_ref[:, span]).astype(jnp.bfloat16)
    square_ref[...] = jnp.broadcast_to(squares, square_ref.shape)
    for copy in copies:
        copy.wait()
    for at in range(0, columns, tile):
        span = slice(at, at + tile)
        acc = dot(x_ref[...], held[:, span], ((1,), (0,)))
        own_ref[:, span] = acc[:rows]
        twin_ref[:, span] = acc[rows:].astype(twin_ref.dtype)


def query_project(ids, states, sums, gain, pieces, count):
    _, shard, columns = pieces[0].shape
    features = states[0].shape[0]
    tokens = sum(s.shape[1] for s in states)
    rows = tokens // CORES
    return pl.pallas_call(
        functools.partial(query_kernel, len(states), len(sums)),
        grid_spec=pltpu.PrefetchScalarGridSpec(
            num_scalar_prefetch=1,
            grid=(1,),
            in_specs=[whole(v) for v in (*states, *sums, gain)] + [pl.BlockSpec(memory_space=pl.ANY)] * len(pieces),
            out_specs=[
                pl.BlockSpec((features, tokens), lambda n, _: (0, 0)),
                pl.BlockSpec((rows, columns), lambda n, _: (0, 0)),
                pl.BlockSpec((rows, columns), lambda n, _: (0, 0)),
                pl.BlockSpec((tokens, 128), lambda n, _: (0, 0)),
            ],
            scratch_shapes=[
                pltpu.VMEM((tokens, features), jnp.bfloat16),
                pltpu.VMEM((features, columns), jnp.bfloat16),
                pltpu.SemaphoreType.DMA((count,)),
            ],
        ),
        out_shape=[
            jax.ShapeDtypeStruct((features, tokens), jnp.float32),
            jax.ShapeDtypeStruct((rows, columns), jnp.float32),
            jax.ShapeDtypeStruct((rows, columns), jnp.bfloat16),
            jax.ShapeDtypeStruct((tokens, 128), jnp.float32),
        ],
        compiler_params=PARAMS,
        cost_estimate=COST,
        name="query_project",
    )(ids, *states, *sums, gain, *pieces)


def listed_kernel(group, width_all, count, seen_ref, qo_ref, qt_ref, so_ref, st_ref, *refs):
    k_refs, v_refs, o_ref = refs[:count], refs[count : 2 * count], refs[2 * count]
    rows = qo_ref.shape[0]
    width = HEAD_WIDTH
    per = 4 if count % 4 == 0 else 1
    factor = lax.rsqrt((so_ref[...] + st_ref[...]) / width_all + EPSILON)
    q = jnp.concatenate(
        [
            (
                (qo_ref[:, g * width : (g + 1) * width] + qt_ref[:, g * width : (g + 1) * width].astype(jnp.float32))
                * factor
            ).astype(jnp.bfloat16)
            for g in range(group)
        ],
        axis=0,
    )
    own_row = lax.broadcasted_iota(jnp.int32, (rows, rows), 0)
    own_col = lax.broadcasted_iota(jnp.int32, (rows, rows), 1)
    causal = jnp.concatenate([own_col <= own_row] * group, axis=0)
    parts = []
    for start in range(0, count, per):
        keys = jnp.concatenate([ref[...] for ref in k_refs[start : start + per]], axis=0)
        s = dot(q, keys, ((1,), (1,)))
        pieces = []
        for i in range(per):
            piece = s[:, i * rows : (i + 1) * rows]
            allowed = causal if start + i == 0 else seen_ref[start + i] > 0
            pieces.append(jnp.where(allowed, piece, MASKED))
        parts.append(jnp.concatenate(pieces, axis=1))
    largest = functools.reduce(jnp.maximum, [jnp.max(p, axis=1, keepdims=True) for p in parts])
    total = jnp.zeros_like(largest)
    acc = jnp.zeros((group * rows, width), jnp.float32)
    for n, p in enumerate(parts):
        weights = jnp.exp2((p - largest) * SCALE)
        total = total + jnp.sum(weights, axis=1, keepdims=True)
        values = jnp.concatenate([ref[...] for ref in v_refs[n * per : (n + 1) * per]], axis=0)
        acc = acc + dot(weights.astype(jnp.bfloat16), values, ((1,), (0,)))
    acc = acc / total
    for g in range(group):
        o_ref[:, g * width : (g + 1) * width] = acc[g * rows : (g + 1) * rows].astype(o_ref.dtype)


def listed_attention(seen, own, brought, squares, twin_squares, blocks, kv_heads, width_all):
    rows, columns = own.shape
    group = columns // (kv_heads * HEAD_WIDTH)
    queries = pl.BlockSpec((rows, group * HEAD_WIDTH), lambda h, _: (0, h))
    sides = pl.BlockSpec((rows, 128), lambda h, _: (0, 0))
    return pl.pallas_call(
        functools.partial(listed_kernel, group, width_all, len(blocks)),
        grid_spec=pltpu.PrefetchScalarGridSpec(
            num_scalar_prefetch=1,
            grid=(kv_heads,),
            in_specs=[queries, queries, sides, sides]
            + [pl.BlockSpec((rows, HEAD_WIDTH), lambda h, _: (0, h)) for _ in blocks]
            + [pl.BlockSpec((rows, HEAD_WIDTH), lambda h, _: (0, kv_heads + h)) for _ in blocks],
            out_specs=queries,
        ),
        out_shape=jax.ShapeDtypeStruct((rows, columns), jnp.bfloat16),
        compiler_params=PARAMS,
        cost_estimate=COST,
        name="listed_attention",
    )(seen, own, brought, squares, twin_squares, *blocks, *blocks)


def output_kernel(ids_ref, own_ref, other_ref, *refs):
    *w_refs, o_ref, held, arrived = refs
    copies = fetch(ids_ref, w_refs, held, arrived)
    context = jnp.concatenate([own_ref[...], other_ref[...]], axis=0)
    shard = held.shape[0] // len(copies)
    for j, copy in enumerate(copies):
        copy.wait()
        at = slice(j * shard, (j + 1) * shard)
        o_ref[at, :] = dot(held[at, :], context, ((1,), (1,))).astype(o_ref.dtype)


def output_project(ids, own, other, pieces, count):
    _, shard, columns = pieces[0].shape
    tokens = own.shape[0] + other.shape[0]
    return pl.pallas_call(
        output_kernel,
        grid_spec=pltpu.PrefetchScalarGridSpec(
            num_scalar_prefetch=1,
            grid=(1,),
            in_specs=[whole(own), whole(other)] + [pl.BlockSpec(memory_space=pl.ANY)] * len(pieces),
            out_specs=pl.BlockSpec((count * shard, tokens), lambda n, _: (0, 0)),
            scratch_shapes=[
                pltpu.VMEM((count * shard, columns), jnp.bfloat16),
                pltpu.SemaphoreType.DMA((count,)),
            ],
        ),
        out_shape=jax.ShapeDtypeStruct((count * shard, tokens), jnp.bfloat16),
        compiler_params=PARAMS,
        cost_estimate=COST,
        name="output_project",
    )(ids, own, other, *pieces)


def last_output_kernel(heads, ids_ref, places_ref, own_ref, other_ref, state_ref, *refs):
    w_refs, refs = refs[: -2 * heads - 2], refs[-2 * heads - 2 :]
    own_refs, twin_refs, held, arrived = refs[:heads], refs[heads : 2 * heads], refs[-2], refs[-1]
    copies = fetch(ids_ref, w_refs, held, arrived)
    context = jnp.concatenate([own_ref[...], other_ref[...]], axis=0)
    rows = own_ref.shape[0]
    shard = held.shape[0] // len(copies)
    share = len(copies) // heads
    for j, copy in enumerate(copies):
        copy.wait()
        at = slice(j * shard, (j + 1) * shard)
        term = dot(held[at, :], context, ((1,), (1,))).astype(jnp.bfloat16)
        place = places_ref[j]
        for k in range(heads):

            @pl.when(place // share == k)
            def _(k=k, term=term, at=at, place=place):
                to = pl.ds(pl.multiple_of((place - k * share) * shard, shard), shard)
                value = state_ref[at, :] + term.astype(jnp.float32) if k == 0 else term
                own_refs[k][to, :] = value[:, :rows]
                twin_refs[k][to, :] = value[:, rows:]


def last_output_project(ids, places, own, other, state, pieces, count, heads):
    _, shard, columns = pieces[0].shape
    rows = own.shape[0]
    held = (count // heads * shard, rows)
    return pl.pallas_call(
        functools.partial(last_output_kernel, heads),
        grid_spec=pltpu.PrefetchScalarGridSpec(
            num_scalar_prefetch=2,
            grid=(1,),
            in_specs=[whole(own), whole(other), whole(state)] + [pl.BlockSpec(memory_space=pl.ANY)] * len(pieces),
            out_specs=[pl.BlockSpec(held, lambda n, *_: (0, 0))] * (2 * heads),
            scratch_shapes=[
                pltpu.VMEM((count * shard, columns), jnp.bfloat16),
                pltpu.SemaphoreType.DMA((count,)),
            ],
        ),
        out_shape=[
            jax.ShapeDtypeStruct(held, jnp.float32 if k == 0 else jnp.bfloat16) for _ in range(2) for k in range(heads)
        ],
        compiler_params=PARAMS,
        cost_estimate=COST,
        name="last_output_project",
    )(ids, places, own, other, state, *pieces)


def result_kernel(heads, shard, at_ref, *refs):
    own, twin, (o_ref, turned) = refs[:heads], refs[heads : 2 * heads], refs[2 * heads :]
    count = own[0].shape[0] // shard
    for k, sums in enumerate((own, twin)):
        for j in range(count):
            span = slice(j * shard, (j + 1) * shard)
            to = pl.ds(pl.multiple_of(at_ref[k * count + j] * shard, shard), shard)
            turned[to, :] = added([ref[span, :] for ref in sums])
    o_ref[...] = turned[...].T


def arrange(at, own, twin, shard):
    features, rows = own[0].shape
    return pl.pallas_call(
        functools.partial(result_kernel, len(own), shard),
        grid_spec=pltpu.PrefetchScalarGridSpec(
            num_scalar_prefetch=1,
            grid=(1,),
            in_specs=[whole(v) for v in (*own, *twin)],
            out_specs=pl.BlockSpec((rows, CORES * features), lambda n, _: (0, 0)),
            scratch_shapes=[pltpu.VMEM((CORES * features, rows), jnp.float32)],
        ),
        out_shape=jax.ShapeDtypeStruct((rows, CORES * features), jnp.float32),
        compiler_params=PARAMS,
        cost_estimate=COST,
        name="arrange",
    )(at, *own, *twin)


def body(
    tokens,
    norm_gains,
    window,
    self_query,
    self_key_value,
    self_output,
    shared_key_value,
    cross_query,
    cross_output,
    key_blocks,
):
    seq_count = lax.axis_size("seq")
    head_count = lax.axis_size("head")
    seq_rank = lax.axis_index("seq")
    head_rank = lax.axis_index("head")
    rows = tokens.shape[0]
    model_width = self_query.shape[0]
    kv_heads = self_key_value.shape[2] // HEAD_WIDTH
    sections, shard = cross_query.shape[:2]
    chips = seq_count // CORES

    order = list(range(0, chips, 2)) + list(range(1, chips, 2))[::-1]
    place = np.argsort(np.array(order))
    rightward, leftward = [], []
    for core in range(CORES):
        ranks = [chip * CORES + core for chip in order]
        rightward += [(ranks[i], ranks[(i + 1) % chips]) for i in range(chips)]
        leftward += [(ranks[i], ranks[i - 1]) for i in range(chips)]
    twins = [(rank, rank ^ 1) for rank in range(seq_count)]

    my_core = seq_rank % CORES
    my_place = jnp.take(jnp.asarray(place, jnp.int32), seq_rank // CORES)
    ring_chips = jnp.take(jnp.asarray(order, jnp.int32), (my_place + jnp.arange(chips)) % chips)
    own_shards = ring_chips * CORES + my_core
    twin_shards = ring_chips * CORES + (1 - my_core)

    def to_twin(value):
        return lax.ppermute(value, "seq", twins)

    def head_shift(value, k):
        return lax.ppermute(value, "head", [(i, (i + k) % head_count) for i in range(head_count)])

    def over_heads(value):
        return [value] + [head_shift(value, k) for k in range(1, head_count)]

    events, hops, found = {}, {}, {}

    def tied(value, name):
        needed = [hop(*at) for at in DONE_BEFORE.get(name, ())]
        if not needed or not jax.tree.leaves(value):
            return value
        return lax.optimization_barrier((value, needed))[0]

    def hop(chain, step):
        if (chain, step) in hops:
            return hops[chain, step]
        more_right = chain % 2 == 0
        right = chips // 2 if more_right else chips - 1 - chips // 2
        left = chips - 1 - right
        if step == 0:
            value = chains[chain]
            found[chain] = {0: value}
            values = [value, value]
        else:
            values = list(hop(chain, step - 1))
        after = START_AFTER.get((chain, step))
        if after is not None:
            after = events[after] if isinstance(after, str) else hop(*after)
            values, _ = lax.optimization_barrier((values, after))
        if step < right:
            values[0] = lax.ppermute(values[0], "seq", rightward)
            found[chain][-(step + 1) % chips] = values[0]
        if step < left:
            values[1] = lax.ppermute(values[1], "seq", leftward)
            found[chain][step + 1] = values[1]
        hops[chain, step] = tuple(values)
        return hops[chain, step]

    def pieces_of(chain):
        for step in range(chips // 2):
            hop(chain, step)
        return [found[chain][j] for j in range(chips)]

    early = lax.all_gather(jnp.stack([cross_query[0], cross_output[0].T]), "seq")
    early = early.reshape(-1, *cross_query.shape[1:])
    chains = {}
    for s in range(1, sections):
        chains[2 * s - 2] = cross_query[s][None]
        chains[2 * s - 1] = cross_output[s].T[None]

    def weights_of(section, which):
        if section == 0:
            return 2 * own_shards + which, [early]
        return jnp.zeros_like(own_shards), pieces_of(2 * section - 2 + which)

    held = over_heads(tokens)
    parts = []
    for j in range(head_count):
        part = held[0]
        for k in range(1, head_count):
            part = jnp.where((head_rank - j) % head_count == k, held[k], part)
        parts.append(part)

    first, own_pair = norm_and_pair(parts, norm_gains[0:1], self_key_value)
    before = lax.ppermute(own_pair, "seq", [(i, i + 1) for i in range(seq_count - 1)])
    query = product(first, self_query)
    info = jnp.concatenate([seq_rank.reshape(1).astype(jnp.int32), window])
    context = window_attention(info, query, before, own_pair, kv_heads)
    sums = over_heads(product(context, self_output))

    ids = jnp.concatenate([own_shards, twin_shards])
    own_cache, mine, others = cache_and_state(ids, parts, sums, norm_gains[1:2], shared_key_value, chips)
    chains[CACHE] = own_cache
    own_blocks = pieces_of(CACHE)
    blocks = own_blocks + [to_twin(block) for block in own_blocks]
    at_blocks = jnp.concatenate([own_shards, twin_shards])
    seen = jnp.any(key_blocks[:, 0, :, None] == at_blocks[None, None, :], axis=1).astype(jnp.int32)
    states, sums = [mine, to_twin(others)], []
    gains = jnp.take(norm_gains.reshape(-1, seq_count, shard), own_shards, axis=1).reshape(-1, chips * shard)

    for s in range(sections):
        sums = tied(sums, f"y{s}")
        states = tied(states, f"q{s}")
        at, query_pieces = weights_of(s, 0)
        state, own, for_twin, squares = query_project(at, states, sums, gains[2 + s][None], query_pieces, chips)
        events[f"q{s}"] = for_twin
        brought = to_twin(for_twin)
        twin_squares = to_twin(squares[rows:])
        brought = tied(brought, f"a{s}")
        own = listed_attention(
            seen[s], own, brought, squares[:rows], twin_squares, blocks, kv_heads, model_width
        )
        events[f"a{s}"] = own
        own = tied(own, f"t{s}")
        other = to_twin(own)
        other = tied(other, f"o{s}")
        at, output_pieces = weights_of(s, 1)
        if s < sections - 1:
            partial = output_project(at, own, other, output_pieces, chips)
            events[f"o{s}"] = partial
            states, sums = [state], over_heads(partial)

    per_head = seq_count // head_count
    share = chips // head_count
    of_head = own_shards // per_head
    ranks = jnp.arange(chips)
    before_it = (of_head[None, :] == of_head[:, None]) & (ranks[None, :] < ranks[:, None])
    slots = jnp.sum(before_it, axis=1, dtype=jnp.int32)
    head_slots = (of_head - head_rank) % head_count * share + slots
    parts = last_output_project(at, head_slots, own, other, state, output_pieces, chips, head_count)
    own_parts, twin_parts = list(parts[:head_count]), parts[head_count:]
    twin_parts = [to_twin(part) for part in twin_parts]
    for k in range(1, head_count):
        own_parts[k] = head_shift(own_parts[k], k)
        twin_parts[k] = head_shift(twin_parts[k], k)
    columns = jnp.sum(
        jnp.where((head_slots[None, :] == jnp.arange(share)[:, None]), own_shards[None, :], 0), axis=1, dtype=jnp.int32
    )
    columns = columns - head_rank * per_head
    other_columns = columns + 1 - 2 * my_core
    return arrange(jnp.concatenate([columns, other_columns]), own_parts, twin_parts, shard)


CACHE = -2
START_AFTER = {(0, 0): (CACHE, 3), (1, 0): (CACHE, 3), (2, 0): (1, 1), (3, 0): (2, 1)}
DONE_BEFORE = {"q0": [(CACHE, 3)]}


def solution(mesh):
    placed = (
        P("seq", "head"),
        P(),
        P("head"),
        P(None, "head"),
        P(None, None, "head"),
        P("head", None),
        P(None, None, "head"),
        P(None, "seq", "head"),
        P(None, "head", "seq"),
        P(None, "seq", None),
    )
    return jax.shard_map(body, mesh=mesh, in_specs=placed, out_specs=P("seq", "head"), check_vma=False)
```

time: 615 us -> 354 us (0.58); the launches traced: 608 us -> 353 us
  waiting for transfers between devices: 379 us -> 145 us
  Pallas kernels: 0 us -> 96.2 us
  matrix products: 85.1 us -> 0 us
  starting transfers between devices: 6.16 us -> 69.8 us
  blocking collectives: 48.5 us -> 0 us
  other arithmetic: 29.1 us -> 1.97 us
  local copies, waits for them, and re-layouts: 45.5 us -> 25.2 us
    all_gather x4 -> x1, waiting for transfers between devices: 329 us -> 0.01 us  [body(): lax.all_gather(jnp.stack([cross_query[0], cross_output[0].T]), 'seq')]
    ppermute x2 -> x62, waiting for transfers between devices: 0.01 us -> 145 us  [the longest x18 74.7 us: hop(): values[0] = lax.ppermute(values[0], 'seq', rightward)]
    pallas_call x0 -> x15, Pallas kernels: none -> 96.2 us  [the longest x3 33.5 us: listed_attention(): pl.pallas_call(functools.partial(listed_kernel, group, width_all, len(blo...]
    dot_general x19 -> x0, matrix products: 84.3 us -> none  [the longest x8 31.1 us: project(): jnp.dot(inputs, weight, preferred_element_type=jnp.float32)]
    ppermute x2 -> x62, starting transfers between devices: 5.87 us -> 69.8 us  [the longest x18 31 us: hop(): values[0] = lax.ppermute(values[0], 'seq', rightward)]
    reduce_scatter x4 -> x0, waiting for transfers between devices: 48.7 us -> none  [add_branch(): lax.psum_scatter(partial_value.astype(jnp.bfloat16), 'head', scatter_dime...]
    all_gather x4 -> x0, blocking collectives: 48.5 us -> none  [normed_full(): lax.all_gather(stream.astype(jnp.float32).astype(jnp.bfloat16), 'head', a...]
    another operation x6 -> x2, local copies, waits for them, and re-layouts: 20.5 us -> 0.61 us  [the longest x1 0.61 us: body(): my_place = jnp.take(jnp.asarray(place, jnp.int32), seq_rank // CORES)]
  transfers between devices with their start and end apart: 10 -> 63, of which waited for: 7 -> 30; matrix products, arithmetic and copies ran while one was open for 13% -> 2% of each run, Pallas kernels for 0% -> 25%
where the time goes in v2:
time: 354 us; the launch traced here: 353 us
  waiting for transfers between devices  145 us (41%)
  Pallas kernels  96.2 us (27%)
  starting transfers between devices  69.8 us (20%)
  local copies, waits for them, and re-layouts  25.2 us (7%)
  between operations  14.5 us (4%)
    ppermute x18, waiting for transfers between devices, hop(): values[0] = lax.ppermute(values[0], 'seq', rightward)  74.7 us
    ppermute x17, waiting for transfers between devices, hop(): values[1] = lax.ppermute(values[1], 'seq', leftward)  38 us
    pallas_call x3, Pallas kernels, listed_attention(): pl.pallas_call(functools.partial(listed_kernel, group, width_all, len(blo...  33.5 us
    ppermute x18, starting transfers between devices, hop(): values[0] = lax.ppermute(values[0], 'seq', rightward)  31 us
    ppermute x6, waiting for transfers between devices, head_shift(): lax.ppermute(value, 'head', [(i, (i + k) % head_count) for i in range(hea...  28.7 us
    ppermute x17, starting transfers between devices, hop(): values[1] = lax.ppermute(values[1], 'seq', leftward)  24.3 us
    pallas_call x3, Pallas kernels, query_project(): pl.pallas_call(functools.partial(query_kernel, len(states), len(sums)), g...  17.7 us
    unnamed x49, local copies, waits for them, and re-layouts  15.6 us
  transfers between devices with their start and end apart: 63, of which 30 were waited for; matrix products, arithmetic and copies ran while one was open for 2% of the time, Pallas kernels for 25%

profile of v2, /device:TPU:0, one launch (start us, length us, event | category | flops | bytes accessed | tf_op | source)
XLA Modules:
  0.0 353.0 jit_solution(6326108393443624750)
XLA Ops:
  6.5 2.7 slice_bitcast_fusion
  9.2 1.2 fusion.10
  11.5 3.0 collective-permute-start
  15.5 8.1 %collective-permute-done = bf16[128,1536]{1,0:T(8,128)(2,1)S(1)} collective-permute-done((bf16[128,1536]{1,0:T(8,128)(2,1)S(1)}, bf16[128,1536]{1,0:T(8,128)(2,1)S(1)}, u32[]{:S(2)}, u32[]{:S(2)}) %collective-permute-start) | collective-permute-done | bytes 393248 | tf_op jit(solution)/shard_map/ppermute | solution.py:488
  23.7 2.8 copy-done
  26.5 2.4 norm_and_pair.1
  28.9 1.3 collective-permute-start.1
  30.3 5.3 %product.2.q_ref = bf16[128,1536]{1,0:T(8,128)(2,1)S(1)} custom-call(bf16[128,3072]{1,0:T(8,128)(2,1)S(1)} %get-tuple-element.36.x_ref, bf16[3072,1536]{1,0:T(8,128)(2,1)} %w_ref.2), custom_call_target="tpu_custom_call" | custom-call | flops 1 | bytes 1 | tf_op jit(solution)/shard_map/product/pallas_call | solution.py:81
  35.6 2.7 window_attention.1.x_ref
  38.4 5.4 %product.3.refs_2_ = bf16[128,3072]{1,0:T(8,128)(2,1)S(1)} custom-call(bf16[128,1536]{1,0:T(8,128)(2,1)S(1)} %window_attention.1.x_ref, bf16[1536,3072]{1,0:T(8,128)(2,1)} %w_ref.3), custom_call_target="tpu_custom_call" | custom-call | flops 1 | bytes 1 | tf_op jit(solution)/shard_map/product/pallas_call | solution.py:81
  43.8 1.8 collective-permute-start.2
  47.6 11.6 %collective-permute-done.2.refs_3_ = bf16[128,3072]{1,0:T(8,128)(2,1)S(1)} collective-permute-done((bf16[128,3072]{1,0:T(8,128)(2,1)S(1)}, bf16[128,3072]{1,0:T(8,128)(2,1)S(1)}, u32[]{:S(2)}, u32[]{:S(2)}) %collective-permute-start.2) | collective-permute-done | bytes 786464 | tf_op jit(solution)/shard_map/ppermute | solution.py:488
  59.2 6.7 %cache_and_state.1 = (bf16[128,1024]{1,0:T(8,128)(2,1)S(1)}, f32[1536,128]{1,0:T(8,128)S(1)}, f32[1536,128]{1,0:T(8,128)}) custom-call(s32[16]{0:T(128)S(1)} %pad_add_fusion.1.ids_ref, bf16[128,1536]{1,0:T(8,128)(2,1)S(1)} %get-tuple-element.102.refs_0_, bf16[128,1536]{1,0:T(8,128)(2,1)S(1)} %get-tuple-element.101.refs_1_, ...), custom_call_target="tpu_custom_call" | custom-call | flops 1 | bytes 1 | tf_op jit(solution)/shard_map/cache_and_state/pallas_call | solution.py:164
  66.7 8.1 %collective-permute-start.4 = (bf16[128,1024]{1,0:T(8,128)(2,1)S(1)}, bf16[128,1024]{1,0:T(8,128)(2,1)S(1)}, u32[]{:S(2)}, u32[]{:S(2)}) collective-permute-start(bf16[128,1024]{1,0:T(8,128)(2,1)S(1)} %get-tuple-element.40.refs_0_.refs_16_), channel_id=1, source_target_pairs={{0,8},{8,16},{16,24},{24,28},{28,20},{20,12},{12,4},{4,0},{2,10},{... | collective-permute-start | bytes 786440 | tf_op jit(solution)/shard_map/ppermute | solution.py:518
  74.8 3.6 %collective-permute-start.8 = (bf16[128,1024]{1,0:T(8,128)(2,1)S(1)}, bf16[128,1024]{1,0:T(8,128)(2,1)S(1)}, u32[]{:S(2)}, u32[]{:S(2)}) collective-permute-start(bf16[128,1024]{1,0:T(8,128)(2,1)S(1)} %get-tuple-element.40.refs_0_.refs_16_), channel_id=1, source_target_pairs={{0,4},{8,0},{16,8},{24,16},{28,24},{20,28},{12,20},{4,12},{2,6},{1... | collective-permute-start | bytes 786440 | tf_op jit(solution)/shard_map/ppermute | solution.py:521
  78.4 11.9 %collective-permute-done.4.refs_7_.refs_23_ = bf16[128,1024]{1,0:T(8,128)(2,1)S(1)} collective-permute-done((bf16[128,1024]{1,0:T(8,128)(2,1)S(1)}, bf16[128,1024]{1,0:T(8,128)(2,1)S(1)}, u32[]{:S(2)}, u32[]{:S(2)}) %collective-permute-start.4) | collective-permute-done | bytes 262176 | tf_op jit(solution)/shard_map/ppermute | solution.py:518
  90.3 2.0 collective-permute-start.9
  92.4 11.8 %collective-permute-done.5.refs_6_.refs_22_ = bf16[128,1024]{1,0:T(8,128)(2,1)S(1)} collective-permute-done((bf16[128,1024]{1,0:T(8,128)(2,1)S(1)}, bf16[128,1024]{1,0:T(8,128)(2,1)S(1)}, u32[]{:S(2)}, u32[]{:S(2)}) %collective-permute-start.5) | collective-permute-done | bytes 262176 | tf_op jit(solution)/shard_map/ppermute | solution.py:518
  106.2 11.8 %collective-permute-done.6.refs_5_.refs_21_ = bf16[128,1024]{1,0:T(8,128)(2,1)S(1)} collective-permute-done((bf16[128,1024]{1,0:T(8,128)(2,1)S(1)}, bf16[128,1024]{1,0:T(8,128)(2,1)S(1)}, u32[]{:S(2)}, u32[]{:S(2)}) %collective-permute-start.6) | collective-permute-done | bytes 262176 | tf_op jit(solution)/shard_map/ppermute | solution.py:518
  118.8 12.6 %collective-permute-done.7.refs_4_.refs_20_ = bf16[128,1024]{1,0:T(8,128)(2,1)S(1)} collective-permute-done((bf16[128,1024]{1,0:T(8,128)(2,1)S(1)}, bf16[128,1024]{1,0:T(8,128)(2,1)S(1)}, u32[]{:S(2)}, u32[]{:S(2)}) %collective-permute-start.7) | collective-permute-done | bytes 262176 | tf_op jit(solution)/shard_map/ppermute | solution.py:518
  131.3 2.4 collective-permute-start.33
  136.0 1.2 collective-permute-start.26
  137.2 6.7 %collective-permute-done.33.refs_1_ = bf16[1,192,1536]{2,1,0:T(8,128)(2,1)} collective-permute-done((bf16[1,192,1536]{2,1,0:T(8,128)(2,1)}, bf16[1,192,1536]{2,1,0:T(8,128)(2,1)}, u32[]{:S(2)}, u32[]{:S(2)}) %collective-permute-start.33) | collective-permute-done | bytes 589856 | tf_op jit(solution)/shard_map/ppermute | solution.py:521
  143.9 2.4 collective-permute-start.34
  146.2 4.0 %collective-permute-done.37.refs_7_ = bf16[1,192,1536]{2,1,0:T(8,128)(2,1)} collective-permute-done((bf16[1,192,1536]{2,1,0:T(8,128)(2,1)}, bf16[1,192,1536]{2,1,0:T(8,128)(2,1)}, u32[]{:S(2)}, u32[]{:S(2)}) %collective-permute-start.37) | collective-permute-done | bytes 589856 | tf_op jit(solution)/shard_map/ppermute | solution.py:518
  152.1 1.5 gather_fusion.1
  154.3 8.6 %collective-permute-done.26.refs_11_ = bf16[1,192,1536]{2,1,0:T(8,128)(2,1)} collective-permute-done((bf16[1,192,1536]{2,1,0:T(8,128)(2,1)}, bf16[1,192,1536]{2,1,0:T(8,128)(2,1)}, u32[]{:S(2)}, u32[]{:S(2)}) %collective-permute-start.26) | collective-permute-done | bytes 589856 | tf_op jit(solution)/shard_map/ppermute | solution.py:518
  163.0 8.8 %collective-permute-done.38.refs_6_ = bf16[1,192,1536]{2,1,0:T(8,128)(2,1)} collective-permute-done((bf16[1,192,1536]{2,1,0:T(8,128)(2,1)}, bf16[1,192,1536]{2,1,0:T(8,128)(2,1)}, u32[]{:S(2)}, u32[]{:S(2)}) %collective-permute-start.38) | collective-permute-done | bytes 589856 | tf_op jit(solution)/shard_map/ppermute | solution.py:518
  173.8 5.9 %query_project.3 = (f32[1536,256]{1,0:T(8,128)S(1)}, f32[128,1536]{1,0:T(8,128)S(1)}, bf16[128,1536]{1,0:T(8,128)(2,1)S(1)}, f32[256,128]{1,0:T(8,128)S(1)}) custom-call(s32[8]{0:T(128)S(1)} %get-tuple-element.114.ids_ref, f32[1536,128]{1,0:T(8,128)S(1)} %copy-done.6, f32[1536,128]{1,0:T(8,128)} %collective-permute-done.3.refs_1_, ...), custom_call_target="tpu_custom_call" | custom-call | flops 1 | bytes 1 | tf_op jit(solution)/shard_map/query_project/pallas_call | solution.py:243
  179.7 1.4 collective-permute-start.41
  181.9 1.5 collective-permute-start.24
  184.0 11.2 %listed_attention.3.own_ref = bf16[128,1536]{1,0:T(8,128)(2,1)S(1)} custom-call(s32[16]{0:T(128)S(1)} %get-tuple-element.112.seen_ref, f32[128,1536]{1,0:T(8,128)S(1)} %get-tuple-element.44.qo_ref, bf16[128,1536]{1,0:T(8,128)(2,1)S(1)} %collective-permute-done.11.qt_ref, f32[128,128]{1,0:T(8,128)S(1)} %get-tuple-element.108.so_ref, ...), custom_call_target="tpu_custom_call" | custom-call | flops 1 | bytes 1 | tf_op jit(solution)/shard_map/listed_attention/pallas_call | solution.py:320
  195.2 2.5 collective-permute-start.28
  197.7 7.2 %output_project.2.refs_1_ = bf16[1536,256]{1,0:T(8,128)(2,1)} custom-call(s32[8]{0:T(128)S(1)} %get-tuple-element.90.ids_ref, bf16[128,1536]{1,0:T(8,128)(2,1)S(1)} %listed_attention.3.own_ref, bf16[128,1536]{1,0:T(8,128)(2,1)S(1)} %collective-permute-done.21.other_ref, bf16[32,192,1536]{2,1,0:T(8,128)(2,1)} %all-gather.3.cloned.1.call-done.refs_3_.refs_0_), custom_call_target="tpu_custom_call" | custom-call | flops 1 | bytes 1 | tf_op jit(solution)/shard_map/output_project/pallas_call | solution.py:351
  205.0 1.5 collective-permute-start.22
  206.5 2.5 collective-permute-start.45
  211.7 2.4 collective-permute-start.29
  214.2 6.2 %collective-permute-done.42.refs_6_ = bf16[1,192,1536]{2,1,0:T(8,128)(2,1)} collective-permute-done((bf16[1,192,1536]{2,1,0:T(8,128)(2,1)S(1)}, bf16[1,192,1536]{2,1,0:T(8,128)(2,1)}, u32[]{:S(2)}, u32[]{:S(2)}) %collective-permute-start.42) | collective-permute-done | bytes 589856 | tf_op jit(solution)/shard_map/ppermute | solution.py:521
  220.4 2.4 collective-permute-start.35
  222.8 1.4 collective-permute-done.45.refs_10_
  225.1 2.4 collective-permute-start.39
  227.5 5.4 %collective-permute-done.25.refs_7_ = bf16[1,192,1536]{2,1,0:T(8,128)(2,1)S(1)} collective-permute-done((bf16[1,192,1536]{2,1,0:T(8,128)(2,1)S(1)}, bf16[1,192,1536]{2,1,0:T(8,128)(2,1)S(1)}, u32[]{:S(2)}, u32[]{:S(2)}) %collective-permute-start.25) | collective-permute-done | bytes 589856 | tf_op jit(solution)/shard_map/ppermute | solution.py:521
  233.8 2.4 collective-permute-start.51
  239.1 6.2 %query_project.4 = (f32[1536,256]{1,0:T(8,128)S(1)}, f32[128,1536]{1,0:T(8,128)S(1)}, bf16[128,1536]{1,0:T(8,128)(2,1)S(1)}, f32[256,128]{1,0:T(8,128)S(1)}) custom-call(s32[8]{0:T(128)S(1)} %broadcast.513.ids_ref, f32[1536,256]{1,0:T(8,128)} %copy-done.3, bf16[1536,256]{1,0:T(8,128)(2,1)} %output_project.2.refs_1_, ...), custom_call_target="tpu_custom_call" | custom-call | flops 1 | bytes 1 | tf_op jit(solution)/shard_map/query_project/pallas_call | solution.py:243
  246.5 2.2 collective-permute-start.36
  250.7 11.2 %listed_attention.4.own_ref = bf16[128,1536]{1,0:T(8,128)(2,1)S(1)} custom-call(s32[16]{0:T(128)S(1)} %get-tuple-element.111.seen_ref, f32[128,1536]{1,0:T(8,128)S(1)} %get-tuple-element.50.qo_ref, bf16[128,1536]{1,0:T(8,128)(2,1)S(1)} %collective-permute-done.30.qt_ref, f32[128,128]{1,0:T(8,128)S(1)} %get-tuple-element.106.so_ref, ...), custom_call_target="tpu_custom_call" | custom-call | flops 1 | bytes 1 | tf_op jit(solution)/shard_map/listed_attention/pallas_call | solution.py:320
  262.0 2.5 collective-permute-start.55
  264.5 4.5 %collective-permute-done.36.refs_4_ = bf16[1,192,1536]{2,1,0:T(8,128)(2,1)S(1)} collective-permute-done((bf16[1,192,1536]{2,1,0:T(8,128)(2,1)}, bf16[1,192,1536]{2,1,0:T(8,128)(2,1)S(1)}, u32[]{:S(2)}, u32[]{:S(2)}) %collective-permute-start.36) | collective-permute-done | bytes 589856 | tf_op jit(solution)/shard_map/ppermute | solution.py:521
  269.0 7.2 %output_project.3.refs_1_ = bf16[1536,256]{1,0:T(8,128)(2,1)} custom-call(s32[8]{0:T(128)S(1)} %broadcast.513.ids_ref, bf16[128,1536]{1,0:T(8,128)(2,1)S(1)} %listed_attention.4.own_ref, bf16[128,1536]{1,0:T(8,128)(2,1)S(1)} %collective-permute-done.32.other_ref, bf16[1,192,1536]{2,1,0:T(8,128)(2,1)} %get-tuple-element.54.refs_0_, ...), custom_call_target="tpu_custom_call" | custom-call | flops 1 | bytes 1 | tf_op jit(solution)/shard_map/output_project/pallas_call | solution.py:351
  276.2 1.4 collective-permute-start.40
  277.7 2.5 collective-permute-start.43
  280.2 1.2 collective-permute-start.47
  281.4 3.2 collective-permute-start.56
  284.7 11.2 %collective-permute-done.43.refs_7_ = bf16[1,192,1536]{2,1,0:T(8,128)(2,1)} collective-permute-done((bf16[1,192,1536]{2,1,0:T(8,128)(2,1)}, bf16[1,192,1536]{2,1,0:T(8,128)(2,1)}, u32[]{:S(2)}, u32[]{:S(2)}) %collective-permute-start.43) | collective-permute-done | bytes 589856 | tf_op jit(solution)/shard_map/ppermute | solution.py:521
  295.9 1.2 collective-permute-done.47.refs_8_
  301.4 5.7 %query_project.5 = (f32[1536,256]{1,0:T(8,128)S(1)}, f32[128,1536]{1,0:T(8,128)S(1)}, bf16[128,1536]{1,0:T(8,128)(2,1)S(1)}, f32[256,128]{1,0:T(8,128)S(1)}) custom-call(s32[8]{0:T(128)S(1)} %broadcast.513.ids_ref, f32[1536,256]{1,0:T(8,128)} %copy-done.4, bf16[1536,256]{1,0:T(8,128)(2,1)} %output_project.3.refs_1_, ...), custom_call_target="tpu_custom_call" | custom-call | flops 1 | bytes 1 | tf_op jit(solution)/shard_map/query_project/pallas_call | solution.py:243
  307.2 2.1 collective-permute-start.57
  311.0 11.2 %listed_attention.5.own_ref = bf16[128,1536]{1,0:T(8,128)(2,1)S(1)} custom-call(s32[16]{0:T(128)S(1)} %get-tuple-element.113.seen_ref, f32[128,1536]{1,0:T(8,128)S(1)} %get-tuple-element.57.qo_ref, bf16[128,1536]{1,0:T(8,128)(2,1)S(1)} %collective-permute-done.48.qt_ref, f32[128,128]{1,0:T(8,128)S(1)} %get-tuple-element.104.so_ref, ...), custom_call_target="tpu_custom_call" | custom-call | flops 1 | bytes 1 | tf_op jit(solution)/shard_map/listed_attention/pallas_call | solution.py:320
  323.5 2.7 collective-permute-done.54.refs_4_
  326.2 6.4 %last_output_project.1 = (f32[768,128]{1,0:T(8,128)S(1)}, bf16[768,128]{1,0:T(8,128)(2,1)S(1)}, f32[768,128]{1,0:T(8,128)S(1)}, bf16[768,128]{1,0:T(8,128)(2,1)S(1)}) custom-call(s32[8]{0:T(128)S(1)} %broadcast.513.ids_ref, s32[8]{0:T(128)S(1)} %fusion.2.places_ref, bf16[128,1536]{1,0:T(8,128)(2,1)S(1)} %listed_attention.5.own_ref, ...), custom_call_target="tpu_custom_call" | custom-call | flops 1 | bytes 1 | tf_op jit(solution)/shard_map/last_output_project/pallas_call | solution.py:397
  334.1 1.3 collective-permute-start.61
  335.4 5.6 %collective-permute-done.58.refs_1_ = bf16[768,128]{1,0:T(8,128)(2,1)S(1)} collective-permute-done((bf16[768,128]{1,0:T(8,128)(2,1)S(1)}, bf16[768,128]{1,0:T(8,128)(2,1)S(1)}, u32[]{:S(2)}, u32[]{:S(2)}) %collective-permute-start.58) | collective-permute-done | bytes 196640 | tf_op jit(solution)/shard_map/ppermute | solution.py:488
  341.1 3.3 collective-permute-done.61.refs_3_
  344.4 1.8 arrange.1
  (164 shorter events, 35.2 us)
Async XLA Ops:
  6.5 166.1 %all-gather.3.cloned.1.call-start = ((), (), s32[]{:S(2)}) async-start(), calls=%async_computation | async-start | bytes 20054016 | tf_op jit(solution)/shard_map/all_gather | solution.py:531
  11.5 12.1 %collective-permute-start = (bf16[128,1536]{1,0:T(8,128)(2,1)S(1)}, bf16[128,1536]{1,0:T(8,128)(2,1)S(1)}, u32[]{:S(2)}, u32[]{:S(2)}) collective-permute-start(bf16[128,1536]{1,0:T(8,128)(2,1)S(1)} %copy-done.20), channel_id=1, source_target_pairs={{0,1},{1,0},{2,3},{3,2},{4,5},{5,4},{6,7},{7,6},{8,9},{9,8},{10,11... | collective-permute-start | bytes 1179656 | tf_op jit(solution)/shard_map/ppermute | solution.py:488
  28.9 6.7 %collective-permute-start.1 = (bf16[128,1024]{1,0:T(8,128)(2,1)S(1)}, bf16[128,1024]{1,0:T(8,128)(2,1)S(1)}, u32[]{:S(2)}, u32[]{:S(2)}) collective-permute-start(bf16[128,1024]{1,0:T(8,128)(2,1)S(1)} %get-tuple-element.37.ko_ref.vo_ref), channel_id=1, source_target_pairs={{0,2},{2,4},{4,6},{6,8},{8,10},{10,12},{12,14},{14,16},{16,18},{18... | collective-permute-start | bytes 786440 | tf_op jit(solution)/shard_map/ppermute | solution.py:552
  43.8 15.4 %collective-permute-start.2 = (bf16[128,3072]{1,0:T(8,128)(2,1)S(1)}, bf16[128,3072]{1,0:T(8,128)(2,1)S(1)}, u32[]{:S(2)}, u32[]{:S(2)}) collective-permute-start(bf16[128,3072]{1,0:T(8,128)(2,1)S(1)} %product.3.refs_2_), channel_id=1, source_target_pairs={{0,1},{1,0},{2,3},{3,2},{4,5},{5,4},{6,7},{7,6},{8,9},{9,8},{10,11... | collective-permute-start | bytes 2359304 | tf_op jit(solution)/shard_map/ppermute | solution.py:488
  59.2 113.4 %copy-start.21 = (s32[3,1,16]{2,1,0:T(1,128)S(1)}, s32[3,1,16]{2,1,0:T(1,128)}, u32[]{:S(2)}) copy-start(s32[3,1,16]{2,1,0:T(1,128)} %param.21) | copy-start | bytes 580
  66.7 23.6 %collective-permute-start.4 = (bf16[128,1024]{1,0:T(8,128)(2,1)S(1)}, bf16[128,1024]{1,0:T(8,128)(2,1)S(1)}, u32[]{:S(2)}, u32[]{:S(2)}) collective-permute-start(bf16[128,1024]{1,0:T(8,128)(2,1)S(1)} %get-tuple-element.40.refs_0_.refs_16_), channel_id=1, source_target_pairs={{0,8},{8,16},{16,24},{24,28},{28,20},{20,12},{12,4},{4,0},{2,10},{... | collective-permute-start | bytes 786440 | tf_op jit(solution)/shard_map/ppermute | solution.py:518
  74.8 15.5 %collective-permute-start.8 = (bf16[128,1024]{1,0:T(8,128)(2,1)S(1)}, bf16[128,1024]{1,0:T(8,128)(2,1)S(1)}, u32[]{:S(2)}, u32[]{:S(2)}) collective-permute-start(bf16[128,1024]{1,0:T(8,128)(2,1)S(1)} %get-tuple-element.40.refs_0_.refs_16_), channel_id=1, source_target_pairs={{0,4},{8,0},{16,8},{24,16},{28,24},{20,28},{12,20},{4,12},{2,6},{1... | collective-permute-start | bytes 786440 | tf_op jit(solution)/shard_map/ppermute | solution.py:521
  90.3 13.8 %collective-permute-start.5 = (bf16[128,1024]{1,0:T(8,128)(2,1)S(1)}, bf16[128,1024]{1,0:T(8,128)(2,1)S(1)}, u32[]{:S(2)}, u32[]{:S(2)}) collective-permute-start(bf16[128,1024]{1,0:T(8,128)(2,1)S(1)} %collective-permute-done.4.refs_7_.refs_23_), channel_id=1, source_target_pairs={{0,8},{8,16},{16,24},{24,28},{28,20},{20,12},{12,4},{4,0},{2,10},{... | collective-permute-start | bytes 786440 | tf_op jit(solution)/shard_map/ppermute | solution.py:518
  90.3 15.2 %collective-permute-start.9 = (bf16[128,1024]{1,0:T(8,128)(2,1)S(1)}, bf16[128,1024]{1,0:T(8,128)(2,1)S(1)}, u32[]{:S(2)}, u32[]{:S(2)}) collective-permute-start(bf16[128,1024]{1,0:T(8,128)(2,1)S(1)} %collective-permute-done.8.refs_1_.refs_17_), channel_id=1, source_target_pairs={{0,4},{8,0},{16,8},{24,16},{28,24},{20,28},{12,20},{4,12},{2,6},{1... | collective-permute-start | bytes 786440 | tf_op jit(solution)/shard_map/ppermute | solution.py:521
  104.2 13.8 %collective-permute-start.6 = (bf16[128,1024]{1,0:T(8,128)(2,1)S(1)}, bf16[128,1024]{1,0:T(8,128)(2,1)S(1)}, u32[]{:S(2)}, u32[]{:S(2)}) collective-permute-start(bf16[128,1024]{1,0:T(8,128)(2,1)S(1)} %collective-permute-done.5.refs_6_.refs_22_), channel_id=1, source_target_pairs={{0,8},{8,16},{16,24},{24,28},{28,20},{20,12},{12,4},{4,0},{2,10},{... | collective-permute-start | bytes 786440 | tf_op jit(solution)/shard_map/ppermute | solution.py:518
  105.5 13.2 %collective-permute-start.10 = (bf16[128,1024]{1,0:T(8,128)(2,1)S(1)}, bf16[128,1024]{1,0:T(8,128)(2,1)S(1)}, u32[]{:S(2)}, u32[]{:S(2)}) collective-permute-start(bf16[128,1024]{1,0:T(8,128)(2,1)S(1)} %collective-permute-done.9.refs_2_.refs_18_), channel_id=1, source_target_pairs={{0,4},{8,0},{16,8},{24,16},{28,24},{20,28},{12,20},{4,12},{2,6},{1... | collective-permute-start | bytes 786440 | tf_op jit(solution)/shard_map/ppermute | solution.py:521
  118.0 13.3 %collective-permute-start.7 = (bf16[128,1024]{1,0:T(8,128)(2,1)S(1)}, bf16[128,1024]{1,0:T(8,128)(2,1)S(1)}, u32[]{:S(2)}, u32[]{:S(2)}) collective-permute-start(bf16[128,1024]{1,0:T(8,128)(2,1)S(1)} %collective-permute-done.6.refs_5_.refs_21_), channel_id=1, source_target_pairs={{0,8},{8,16},{16,24},{24,28},{28,20},{20,12},{12,4},{4,0},{2,10},{... | collective-permute-start | bytes 786440 | tf_op jit(solution)/shard_map/ppermute | solution.py:518
  131.3 12.6 %collective-permute-start.33 = (bf16[1,192,1536]{2,1,0:T(8,128)(2,1)}, bf16[1,192,1536]{2,1,0:T(8,128)(2,1)}, u32[]{:S(2)}, u32[]{:S(2)}) collective-permute-start(bf16[1,192,1536]{2,1,0:T(8,128)(2,1)} %get-tuple-element.54.refs_0_), channel_id=1, source_target_pairs={{0,4},{8,0},{16,8},{24,16},{28,24},{20,28},{12,20},{4,12},{2,6},{1... | collective-permute-start | bytes 1769480 | tf_op jit(solution)/shard_map/ppermute | solution.py:521
  133.7 16.6 %collective-permute-start.37 = (bf16[1,192,1536]{2,1,0:T(8,128)(2,1)}, bf16[1,192,1536]{2,1,0:T(8,128)(2,1)}, u32[]{:S(2)}, u32[]{:S(2)}) collective-permute-start(bf16[1,192,1536]{2,1,0:T(8,128)(2,1)} %get-tuple-element.54.refs_0_), channel_id=1, source_target_pairs={{0,8},{8,16},{16,24},{24,28},{28,20},{20,12},{12,4},{4,0},{2,10},{... | collective-permute-start | bytes 1769480 | tf_op jit(solution)/shard_map/ppermute | solution.py:518
  133.7 1.5 collective-permute-start.13
  133.7 1.9 collective-permute-start.14
  134.2 1.8 collective-permute-start.20
  135.2 19.0 %collective-permute-start.3 = (f32[1536,128]{1,0:T(8,128)}, f32[1536,128]{1,0:T(8,128)}, u32[]{:S(2)}, u32[]{:S(2)}) collective-permute-start(f32[1536,128]{1,0:T(8,128)} %get-tuple-element.39), channel_id=1, source_target_pairs={{0,2},{2,0},{4,6},{6,4},{8,10},{10,8},{12,14},{14,12},{16,18},{18,... | collective-permute-start | bytes 2359304 | tf_op jit(solution)/shard_map/ppermute | solution.py:485
  135.6 14.7 %collective-permute-start.15 = (bf16[128,1024]{1,0:T(8,128)(2,1)S(1)}, bf16[128,1024]{1,0:T(8,128)(2,1)S(1)}, u32[]{:S(2)}, u32[]{:S(2)}) collective-permute-start(bf16[128,1024]{1,0:T(8,128)(2,1)S(1)} %collective-permute-done.9.refs_2_.refs_18_), channel_id=1, source_target_pairs={{0,2},{2,0},{4,6},{6,4},{8,10},{10,8},{12,14},{14,12},{16,18},{18,... | collective-permute-start | bytes 786440 | tf_op jit(solution)/shard_map/ppermute | solution.py:485
  136.0 26.9 %collective-permute-start.26 = (bf16[1,192,1536]{2,1,0:T(8,128)(2,1)}, bf16[1,192,1536]{2,1,0:T(8,128)(2,1)}, u32[]{:S(2)}, u32[]{:S(2)}) collective-permute-start(bf16[1,192,1536]{2,1,0:T(8,128)(2,1)} %get-tuple-element.48.refs_4_), channel_id=1, source_target_pairs={{0,8},{8,16},{16,24},{24,28},{28,20},{20,12},{12,4},{4,0},{2,10},{... | collective-permute-start | bytes 1769480 | tf_op jit(solution)/shard_map/ppermute | solution.py:518
  143.9 19.0 %collective-permute-start.34 = (bf16[1,192,1536]{2,1,0:T(8,128)(2,1)}, bf16[1,192,1536]{2,1,0:T(8,128)(2,1)}, u32[]{:S(2)}, u32[]{:S(2)}) collective-permute-start(bf16[1,192,1536]{2,1,0:T(8,128)(2,1)} %collective-permute-done.33.refs_1_), channel_id=1, source_target_pairs={{0,4},{8,0},{16,8},{24,16},{28,24},{20,28},{12,20},{4,12},{2,6},{1... | collective-permute-start | bytes 1769480 | tf_op jit(solution)/shard_map/ppermute | solution.py:521
  150.3 21.6 %collective-permute-start.38 = (bf16[1,192,1536]{2,1,0:T(8,128)(2,1)}, bf16[1,192,1536]{2,1,0:T(8,128)(2,1)}, u32[]{:S(2)}, u32[]{:S(2)}) collective-permute-start(bf16[1,192,1536]{2,1,0:T(8,128)(2,1)} %collective-permute-done.37.refs_7_), channel_id=1, source_target_pairs={{0,8},{8,16},{16,24},{24,28},{28,20},{20,12},{12,4},{4,0},{2,10},{... | collective-permute-start | bytes 1769480 | tf_op jit(solution)/shard_map/ppermute | solution.py:518
  150.3 3.3 collective-permute-start.19
  153.7 26.0 %collective-permute-start.16 = (bf16[128,1024]{1,0:T(8,128)(2,1)S(1)}, bf16[128,1024]{1,0:T(8,128)(2,1)}, u32[]{:S(2)}, u32[]{:S(2)}) collective-permute-start(bf16[128,1024]{1,0:T(8,128)(2,1)S(1)} %collective-permute-done.10.refs_3_.refs_19_), channel_id=1, source_target_pairs={{0,2},{2,0},{4,6},{6,4},{8,10},{10,8},{12,14},{14,12},{16,18},{18,... | collective-permute-start | bytes 786440 | tf_op jit(solution)/shard_map/ppermute | solution.py:485
  154.2 27.0 %collective-permute-start.18 = (bf16[128,1024]{1,0:T(8,128)(2,1)S(1)}, bf16[128,1024]{1,0:T(8,128)(2,1)}, u32[]{:S(2)}, u32[]{:S(2)}) collective-permute-start(bf16[128,1024]{1,0:T(8,128)(2,1)S(1)} %collective-permute-done.6.refs_5_.refs_21_), channel_id=1, source_target_pairs={{0,2},{2,0},{4,6},{6,4},{8,10},{10,8},{12,14},{14,12},{16,18},{18,... | collective-permute-start | bytes 786440 | tf_op jit(solution)/shard_map/ppermute | solution.py:485
  162.9 19.0 %collective-permute-start.23 = (bf16[1,192,1536]{2,1,0:T(8,128)(2,1)}, bf16[1,192,1536]{2,1,0:T(8,128)(2,1)}, u32[]{:S(2)}, u32[]{:S(2)}) collective-permute-start(bf16[1,192,1536]{2,1,0:T(8,128)(2,1)} %get-tuple-element.48.refs_4_), channel_id=1, source_target_pairs={{0,4},{8,0},{16,8},{24,16},{28,24},{20,28},{12,20},{4,12},{2,6},{1... | collective-permute-start | bytes 1769480 | tf_op jit(solution)/shard_map/ppermute | solution.py:521
  162.9 18.3 %collective-permute-start.17 = (bf16[128,1024]{1,0:T(8,128)(2,1)S(1)}, bf16[128,1024]{1,0:T(8,128)(2,1)}, u32[]{:S(2)}, u32[]{:S(2)}) collective-permute-start(bf16[128,1024]{1,0:T(8,128)(2,1)S(1)} %collective-permute-done.7.refs_4_.refs_20_), channel_id=1, source_target_pairs={{0,2},{2,0},{4,6},{6,4},{8,10},{10,8},{12,14},{14,12},{16,18},{18,... | collective-permute-start | bytes 786440 | tf_op jit(solution)/shard_map/ppermute | solution.py:485
  171.9 23.4 %collective-permute-start.27 = (bf16[1,192,1536]{2,1,0:T(8,128)(2,1)}, bf16[1,192,1536]{2,1,0:T(8,128)(2,1)}, u32[]{:S(2)}, u32[]{:S(2)}) collective-permute-start(bf16[1,192,1536]{2,1,0:T(8,128)(2,1)} %collective-permute-done.26.refs_11_), channel_id=1, source_target_pairs={{0,8},{8,16},{16,24},{24,28},{28,20},{20,12},{12,4},{4,0},{2,10},{... | collective-permute-start | bytes 1769480 | tf_op jit(solution)/shard_map/ppermute | solution.py:518
  179.7 18.0 %collective-permute-start.41 = (bf16[1,192,1536]{2,1,0:T(8,128)(2,1)S(1)}, bf16[1,192,1536]{2,1,0:T(8,128)(2,1)S(1)}, u32[]{:S(2)}, u32[]{:S(2)}) collective-permute-start(bf16[1,192,1536]{2,1,0:T(8,128)(2,1)S(1)} %copy-done.1), channel_id=1, source_target_pairs={{0,4},{8,0},{16,8},{24,16},{28,24},{20,28},{12,20},{4,12},{2,6},{1... | collective-permute-start | bytes 1769480 | tf_op jit(solution)/shard_map/ppermute | solution.py:521
  181.2 2.8 collective-permute-start.11
  181.2 2.2 collective-permute-start.12
  181.9 27.9 %collective-permute-start.24 = (bf16[1,192,1536]{2,1,0:T(8,128)(2,1)}, bf16[1,192,1536]{2,1,0:T(8,128)(2,1)S(1)}, u32[]{:S(2)}, u32[]{:S(2)}) collective-permute-start(bf16[1,192,1536]{2,1,0:T(8,128)(2,1)} %collective-permute-done.23.refs_5_), channel_id=1, source_target_pairs={{0,4},{8,0},{16,8},{24,16},{28,24},{20,28},{12,20},{4,12},{2,6},{1... | collective-permute-start | bytes 1769480 | tf_op jit(solution)/shard_map/ppermute | solution.py:521
  183.4 23.1 %collective-permute-start.44 = (bf16[1,192,1536]{2,1,0:T(8,128)(2,1)S(1)}, bf16[1,192,1536]{2,1,0:T(8,128)(2,1)S(1)}, u32[]{:S(2)}, u32[]{:S(2)}) collective-permute-start(bf16[1,192,1536]{2,1,0:T(8,128)(2,1)S(1)} %copy-done.1), channel_id=1, source_target_pairs={{0,8},{8,16},{16,24},{24,28},{28,20},{20,12},{12,4},{4,0},{2,10},{... | collective-permute-start | bytes 1769480 | tf_op jit(solution)/shard_map/ppermute | solution.py:518
  195.1 2.6 collective-permute-start.21
  195.2 16.5 %collective-permute-start.28 = (bf16[1,192,1536]{2,1,0:T(8,128)(2,1)}, bf16[1,192,1536]{2,1,0:T(8,128)(2,1)}, u32[]{:S(2)}, u32[]{:S(2)}) collective-permute-start(bf16[1,192,1536]{2,1,0:T(8,128)(2,1)} %collective-permute-done.27.refs_10_), channel_id=1, source_target_pairs={{0,8},{8,16},{16,24},{24,28},{28,20},{20,12},{12,4},{4,0},{2,10},{... | collective-permute-start | bytes 1769480 | tf_op jit(solution)/shard_map/ppermute | solution.py:518
  197.7 22.7 %collective-permute-start.42 = (bf16[1,192,1536]{2,1,0:T(8,128)(2,1)S(1)}, bf16[1,192,1536]{2,1,0:T(8,128)(2,1)}, u32[]{:S(2)}, u32[]{:S(2)}) collective-permute-start(bf16[1,192,1536]{2,1,0:T(8,128)(2,1)S(1)} %collective-permute-done.41.refs_5_), channel_id=1, source_target_pairs={{0,4},{8,0},{16,8},{24,16},{28,24},{20,28},{12,20},{4,12},{2,6},{1... | collective-permute-start | bytes 1769480 | tf_op jit(solution)/shard_map/ppermute | solution.py:521
  205.0 32.1 %collective-permute-start.22 = (bf16[1536,256]{1,0:T(8,128)(2,1)}, bf16[1536,256]{1,0:T(8,128)(2,1)}, u32[]{:S(2)}, u32[]{:S(2)}) collective-permute-start(bf16[1536,256]{1,0:T(8,128)(2,1)} %output_project.2.refs_1_), channel_id=1, source_target_pairs={{0,1},{1,0},{2,3},{3,2},{4,5},{5,4},{6,7},{7,6},{8,9},{9,8},{10,11... | collective-permute-start | bytes 2359304 | tf_op jit(solution)/shard_map/ppermute | solution.py:488
  206.5 17.8 %collective-permute-start.45 = (bf16[1,192,1536]{2,1,0:T(8,128)(2,1)S(1)}, bf16[1,192,1536]{2,1,0:T(8,128)(2,1)S(1)}, u32[]{:S(2)}, u32[]{:S(2)}) collective-permute-start(bf16[1,192,1536]{2,1,0:T(8,128)(2,1)S(1)} %collective-permute-done.44.refs_11_), channel_id=1, source_target_pairs={{0,8},{8,16},{16,24},{24,28},{28,20},{20,12},{12,4},{4,0},{2,10},{... | collective-permute-start | bytes 1769480 | tf_op jit(solution)/shard_map/ppermute | solution.py:518
  209.8 23.2 %collective-permute-start.25 = (bf16[1,192,1536]{2,1,0:T(8,128)(2,1)S(1)}, bf16[1,192,1536]{2,1,0:T(8,128)(2,1)S(1)}, u32[]{:S(2)}, u32[]{:S(2)}) collective-permute-start(bf16[1,192,1536]{2,1,0:T(8,128)(2,1)S(1)} %collective-permute-done.24.refs_6_), channel_id=1, source_target_pairs={{0,4},{8,0},{16,8},{24,16},{28,24},{20,28},{12,20},{4,12},{2,6},{1... | collective-permute-start | bytes 1769480 | tf_op jit(solution)/shard_map/ppermute | solution.py:521
  211.7 25.3 %collective-permute-start.29 = (bf16[1,192,1536]{2,1,0:T(8,128)(2,1)}, bf16[1,192,1536]{2,1,0:T(8,128)(2,1)}, u32[]{:S(2)}, u32[]{:S(2)}) collective-permute-start(bf16[1,192,1536]{2,1,0:T(8,128)(2,1)} %collective-permute-done.28.refs_9_), channel_id=1, source_target_pairs={{0,8},{8,16},{16,24},{24,28},{28,20},{20,12},{12,4},{4,0},{2,10},{... | collective-permute-start | bytes 1769480 | tf_op jit(solution)/shard_map/ppermute | solution.py:518
  220.4 26.1 %collective-permute-start.35 = (bf16[1,192,1536]{2,1,0:T(8,128)(2,1)}, bf16[1,192,1536]{2,1,0:T(8,128)(2,1)}, u32[]{:S(2)}, u32[]{:S(2)}) collective-permute-start(bf16[1,192,1536]{2,1,0:T(8,128)(2,1)} %collective-permute-done.34.refs_2_), channel_id=1, source_target_pairs={{0,4},{8,0},{16,8},{24,16},{28,24},{20,28},{12,20},{4,12},{2,6},{1... | collective-permute-start | bytes 1769480 | tf_op jit(solution)/shard_map/ppermute | solution.py:521
  225.1 36.9 %collective-permute-start.39 = (bf16[1,192,1536]{2,1,0:T(8,128)(2,1)}, bf16[1,192,1536]{2,1,0:T(8,128)(2,1)}, u32[]{:S(2)}, u32[]{:S(2)}) collective-permute-start(bf16[1,192,1536]{2,1,0:T(8,128)(2,1)} %collective-permute-done.38.refs_6_), channel_id=1, source_target_pairs={{0,8},{8,16},{16,24},{24,28},{28,20},{20,12},{12,4},{4,0},{2,10},{... | collective-permute-start | bytes 1769480 | tf_op jit(solution)/shard_map/ppermute | solution.py:518
  233.8 30.8 %collective-permute-start.51 = (bf16[1,192,1536]{2,1,0:T(8,128)(2,1)}, bf16[1,192,1536]{2,1,0:T(8,128)(2,1)}, u32[]{:S(2)}, u32[]{:S(2)}) collective-permute-start(bf16[1,192,1536]{2,1,0:T(8,128)(2,1)} %get-tuple-element.62.refs_0_), channel_id=1, source_target_pairs={{0,4},{8,0},{16,8},{24,16},{28,24},{20,28},{12,20},{4,12},{2,6},{1... | collective-permute-start | bytes 1769480 | tf_op jit(solution)/shard_map/ppermute | solution.py:521
  246.5 4.3 %collective-permute-start.30 = (bf16[128,1536]{1,0:T(8,128)(2,1)S(1)}, bf16[128,1536]{1,0:T(8,128)(2,1)S(1)}, u32[]{:S(2)}, u32[]{:S(2)}) collective-permute-start(bf16[128,1536]{1,0:T(8,128)(2,1)S(1)} %get-tuple-element.51), channel_id=1, source_target_pairs={{0,2},{2,0},{4,6},{6,4},{8,10},{10,8},{12,14},{14,12},{16,18},{18,... | collective-permute-start | bytes 1179656 | tf_op jit(solution)/shard_map/ppermute | solution.py:485
  246.5 22.5 %collective-permute-start.36 = (bf16[1,192,1536]{2,1,0:T(8,128)(2,1)}, bf16[1,192,1536]{2,1,0:T(8,128)(2,1)S(1)}, u32[]{:S(2)}, u32[]{:S(2)}) collective-permute-start(bf16[1,192,1536]{2,1,0:T(8,128)(2,1)} %collective-permute-done.35.refs_3_), channel_id=1, source_target_pairs={{0,4},{8,0},{16,8},{24,16},{28,24},{20,28},{12,20},{4,12},{2,6},{1... | collective-permute-start | bytes 1769480 | tf_op jit(solution)/shard_map/ppermute | solution.py:521
  248.8 1.3 collective-permute-start.31
  250.1 30.1 %collective-permute-start.46 = (bf16[1,192,1536]{2,1,0:T(8,128)(2,1)S(1)}, bf16[1,192,1536]{2,1,0:T(8,128)(2,1)}, u32[]{:S(2)}, u32[]{:S(2)}) collective-permute-start(bf16[1,192,1536]{2,1,0:T(8,128)(2,1)S(1)} %copy-done.12), channel_id=1, source_target_pairs={{0,8},{8,16},{16,24},{24,28},{28,20},{20,12},{12,4},{4,0},{2,10},{... | collective-permute-start | bytes 1769480 | tf_op jit(solution)/shard_map/ppermute | solution.py:518
  261.9 7.1 %collective-permute-start.32 = (bf16[128,1536]{1,0:T(8,128)(2,1)S(1)}, bf16[128,1536]{1,0:T(8,128)(2,1)S(1)}, u32[]{:S(2)}, u32[]{:S(2)}) collective-permute-start(bf16[128,1536]{1,0:T(8,128)(2,1)S(1)} %listed_attention.4.own_ref), channel_id=1, source_target_pairs={{0,2},{2,0},{4,6},{6,4},{8,10},{10,8},{12,14},{14,12},{16,18},{18,... | collective-permute-start | bytes 1179656 | tf_op jit(solution)/shard_map/ppermute | solution.py:485
  262.0 19.4 %collective-permute-start.55 = (bf16[1,192,1536]{2,1,0:T(8,128)(2,1)}, bf16[1,192,1536]{2,1,0:T(8,128)(2,1)}, u32[]{:S(2)}, u32[]{:S(2)}) collective-permute-start(bf16[1,192,1536]{2,1,0:T(8,128)(2,1)} %get-tuple-element.62.refs_0_), channel_id=1, source_target_pairs={{0,8},{8,16},{16,24},{24,28},{28,20},{20,12},{12,4},{4,0},{2,10},{... | collective-permute-start | bytes 1769480 | tf_op jit(solution)/shard_map/ppermute | solution.py:518
  264.5 20.1 %collective-permute-start.52 = (bf16[1,192,1536]{2,1,0:T(8,128)(2,1)}, bf16[1,192,1536]{2,1,0:T(8,128)(2,1)}, u32[]{:S(2)}, u32[]{:S(2)}) collective-permute-start(bf16[1,192,1536]{2,1,0:T(8,128)(2,1)} %collective-permute-done.51.refs_1_), channel_id=1, source_target_pairs={{0,4},{8,0},{16,8},{24,16},{28,24},{20,28},{12,20},{4,12},{2,6},{1... | collective-permute-start | bytes 1769480 | tf_op jit(solution)/shard_map/ppermute | solution.py:521
  276.2 20.9 %collective-permute-start.40 = (bf16[1536,256]{1,0:T(8,128)(2,1)}, bf16[1536,256]{1,0:T(8,128)(2,1)}, u32[]{:S(2)}, u32[]{:S(2)}) collective-permute-start(bf16[1536,256]{1,0:T(8,128)(2,1)} %output_project.3.refs_1_), channel_id=1, source_target_pairs={{0,1},{1,0},{2,3},{3,2},{4,5},{5,4},{6,7},{7,6},{8,9},{9,8},{10,11... | collective-permute-start | bytes 2359304 | tf_op jit(solution)/shard_map/ppermute | solution.py:488
  277.7 18.3 %collective-permute-start.43 = (bf16[1,192,1536]{2,1,0:T(8,128)(2,1)}, bf16[1,192,1536]{2,1,0:T(8,128)(2,1)}, u32[]{:S(2)}, u32[]{:S(2)}) collective-permute-start(bf16[1,192,1536]{2,1,0:T(8,128)(2,1)} %collective-permute-done.42.refs_6_), channel_id=1, source_target_pairs={{0,4},{8,0},{16,8},{24,16},{28,24},{20,28},{12,20},{4,12},{2,6},{1... | collective-permute-start | bytes 1769480 | tf_op jit(solution)/shard_map/ppermute | solution.py:521
  280.2 16.9 %collective-permute-start.47 = (bf16[1,192,1536]{2,1,0:T(8,128)(2,1)}, bf16[1,192,1536]{2,1,0:T(8,128)(2,1)}, u32[]{:S(2)}, u32[]{:S(2)}) collective-permute-start(bf16[1,192,1536]{2,1,0:T(8,128)(2,1)} %collective-permute-done.46.refs_9_), channel_id=1, source_target_pairs={{0,8},{8,16},{16,24},{24,28},{28,20},{20,12},{12,4},{4,0},{2,10},{... | collective-permute-start | bytes 1769480 | tf_op jit(solution)/shard_map/ppermute | solution.py:518
  281.4 25.8 %collective-permute-start.56 = (bf16[1,192,1536]{2,1,0:T(8,128)(2,1)}, bf16[1,192,1536]{2,1,0:T(8,128)(2,1)}, u32[]{:S(2)}, u32[]{:S(2)}) collective-permute-start(bf16[1,192,1536]{2,1,0:T(8,128)(2,1)} %collective-permute-done.55.refs_7_), channel_id=1, source_target_pairs={{0,8},{8,16},{16,24},{24,28},{28,20},{20,12},{12,4},{4,0},{2,10},{... | collective-permute-start | bytes 1769480 | tf_op jit(solution)/shard_map/ppermute | solution.py:518
  284.6 24.6 %collective-permute-start.53 = (bf16[1,192,1536]{2,1,0:T(8,128)(2,1)}, bf16[1,192,1536]{2,1,0:T(8,128)(2,1)}, u32[]{:S(2)}, u32[]{:S(2)}) collective-permute-start(bf16[1,192,1536]{2,1,0:T(8,128)(2,1)} %collective-permute-done.52.refs_2_), channel_id=1, source_target_pairs={{0,4},{8,0},{16,8},{24,16},{28,24},{20,28},{12,20},{4,12},{2,6},{1... | collective-permute-start | bytes 1769480 | tf_op jit(solution)/shard_map/ppermute | solution.py:521
  307.1 3.9 %collective-permute-start.48 = (bf16[128,1536]{1,0:T(8,128)(2,1)S(1)}, bf16[128,1536]{1,0:T(8,128)(2,1)S(1)}, u32[]{:S(2)}, u32[]{:S(2)}) collective-permute-start(bf16[128,1536]{1,0:T(8,128)(2,1)S(1)} %get-tuple-element.58), channel_id=1, source_target_pairs={{0,2},{2,0},{4,6},{6,4},{8,10},{10,8},{12,14},{14,12},{16,18},{18,... | collective-permute-start | bytes 1179656 | tf_op jit(solution)/shard_map/ppermute | solution.py:485
  307.2 16.3 %collective-permute-start.57 = (bf16[1,192,1536]{2,1,0:T(8,128)(2,1)}, bf16[1,192,1536]{2,1,0:T(8,128)(2,1)S(1)}, u32[]{:S(2)}, u32[]{:S(2)}) collective-permute-start(bf16[1,192,1536]{2,1,0:T(8,128)(2,1)} %collective-permute-done.56.refs_6_), channel_id=1, source_target_pairs={{0,8},{8,16},{16,24},{24,28},{28,20},{20,12},{12,4},{4,0},{2,10},{... | collective-permute-start | bytes 1769480 | tf_op jit(solution)/shard_map/ppermute | solution.py:518
  309.2 16.9 %collective-permute-start.54 = (bf16[1,192,1536]{2,1,0:T(8,128)(2,1)}, bf16[1,192,1536]{2,1,0:T(8,128)(2,1)S(1)}, u32[]{:S(2)}, u32[]{:S(2)}) collective-permute-start(bf16[1,192,1536]{2,1,0:T(8,128)(2,1)} %collective-permute-done.53.refs_3_), channel_id=1, source_target_pairs={{0,4},{8,0},{16,8},{24,16},{28,24},{20,28},{12,20},{4,12},{2,6},{1... | collective-permute-start | bytes 1769480 | tf_op jit(solution)/shard_map/ppermute | solution.py:521
  309.7 1.3 collective-permute-start.49
  322.1 4.0 %collective-permute-start.50 = (bf16[128,1536]{1,0:T(8,128)(2,1)S(1)}, bf16[128,1536]{1,0:T(8,128)(2,1)S(1)}, u32[]{:S(2)}, u32[]{:S(2)}) collective-permute-start(bf16[128,1536]{1,0:T(8,128)(2,1)S(1)} %listed_attention.5.own_ref), channel_id=1, source_target_pairs={{0,2},{2,0},{4,6},{6,4},{8,10},{10,8},{12,14},{14,12},{16,18},{18,... | collective-permute-start | bytes 1179656 | tf_op jit(solution)/shard_map/ppermute | solution.py:485
  332.6 1.5 collective-permute-start.60
  332.6 8.4 %collective-permute-start.59 = (f32[768,128]{1,0:T(8,128)S(1)}, f32[768,128]{1,0:T(8,128)S(1)}, u32[]{:S(2)}, u32[]{:S(2)}) collective-permute-start(f32[768,128]{1,0:T(8,128)S(1)} %get-tuple-element.65), channel_id=1, source_target_pairs={{0,2},{2,0},{4,6},{6,4},{8,10},{10,8},{12,14},{14,12},{16,18},{18,... | collective-permute-start | bytes 1179656 | tf_op jit(solution)/shard_map/ppermute | solution.py:485
  333.3 7.8 %collective-permute-start.58 = (bf16[768,128]{1,0:T(8,128)(2,1)S(1)}, bf16[768,128]{1,0:T(8,128)(2,1)S(1)}, u32[]{:S(2)}, u32[]{:S(2)}) collective-permute-start(bf16[768,128]{1,0:T(8,128)(2,1)S(1)} %get-tuple-element.64), channel_id=1, source_target_pairs={{0,1},{1,0},{2,3},{3,2},{4,5},{5,4},{6,7},{7,6},{8,9},{9,8},{10,11... | collective-permute-start | bytes 589832 | tf_op jit(solution)/shard_map/ppermute | solution.py:488
  334.1 10.3 %collective-permute-start.61 = (bf16[768,128]{1,0:T(8,128)(2,1)S(1)}, bf16[768,128]{1,0:T(8,128)(2,1)S(1)}, u32[]{:S(2)}, u32[]{:S(2)}) collective-permute-start(bf16[768,128]{1,0:T(8,128)(2,1)S(1)} %collective-permute-done.60), channel_id=1, source_target_pairs={{0,1},{1,0},{2,3},{3,2},{4,5},{5,4},{6,7},{7,6},{8,9},{9,8},{10,11... | collective-permute-start | bytes 589832 | tf_op jit(solution)/shard_map/ppermute | solution.py:488
  (23 other events, 78.3 us)
Sparse Core Ops, SparseCore 0:
  11.6 126.3 all-gather.2
